TPU v7x, 32 devices: a whole 2x2x4 slice. The times are simulated.
32 devices in a mesh: groups: 2 (over y), patch: 4 (over z), zbin: 2 (over x), freq: 2 (over core).
Axes of the slice: x: 2, y: 2, z: 4, core: 2. Of those that a mesh axis runs over, the one named last changes fastest.
Arguments:
- density_maps: bfloat16 [8, 4, 1024, 1024], P(('groups', 'patch'), 'zbin', None, 'freq'), parts along dimension 0, may hold values from -6 to 6
- margin_src: int32 [8, 4], P('groups'), parts along dimension 0, may hold values from 0 to 7, as said below
- margin_row: int32 [8, 4], P('groups'), parts along dimension 0, may hold values from 0 to 992
- margin_count: int32 [8], P('groups'), parts along dimension 0, may hold values from 1 to 4
- class_id: int32 [8], P('groups'), parts along dimension 0, may hold values from 0 to 3
- coupling_bank: float32 [4, 128, 128], P('patch'), may hold values from -0.5 to 2
- band_edges: int32 [129], replicated, may hold values from 1 to 511, as said below
Outputs:
- spectra: float32 [8, 10, 128], P(('groups', 'patch'), 'zbin'), parts along dimension 0
There are 2 independent parts, one for each index of `groups`. A program takes and returns all parts, laid end to end along the dimension named above; an argument that names none is the same for every part. Nothing has to cross between parts.
Inputs may be any that keep to these rules, and one draw needn't show every extreme that they name: `margin_src`: entry k of patch p names strip 2 q + s, side s of patch q, where q lies 1 to 1 patches away from p, counted cyclically over the 4 patches. `band_edges`: strictly increasing, the first 1 and the last half of 1024 minus 1.
All inputs are finite; a program needn't handle non-finite values.
Results may differ from a plain program's by a relative error of at most 0.0011.
Values may be sent and summed in bfloat16 or wider, within the bound.
A program may use at most 64 MiB of HBM per device.

v0:
```python
import math

import jax
import jax.numpy as jnp
import numpy as np
from jax import lax
from jax.sharding import PartitionSpec as P

W = 32
APOD = 64
KMAX = 4


def extended(cells, sides, width):
    for axis, dim in sides:
        count = lax.axis_size(axis)
        head = lax.slice_in_dim(cells, 0, width, axis=dim)
        tail = lax.slice_in_dim(cells, cells.shape[dim] - width, cells.shape[dim], axis=dim)
        cells = jnp.concatenate(
            [
                lax.ppermute(tail, axis, [(i, (i + 1) % count) for i in range(count)]),
                cells,
                lax.ppermute(head, axis, [((i + 1) % count, i) for i in range(count)]),
            ],
            axis=dim,
        )
    return cells


def taper_profile(length, ramp_width):
    position = jnp.arange(length, dtype=jnp.int32)
    distance = jnp.minimum(position, length - 1 - position)
    ramped = 0.5 - 0.5 * jnp.cos(math.pi * (distance.astype(jnp.float32) + 0.5) / ramp_width)
    return jnp.where(distance < ramp_width, ramped, jnp.ones_like(ramped))


def fourier_tables(frequencies, samples, length):
    phases = frequencies[:, None] * samples[None, :] % length
    angles = phases.astype(jnp.float32) * (2.0 * math.pi / length)
    return (jnp.cos(angles).astype(jnp.bfloat16), jnp.sin(angles).astype(jnp.bfloat16))


def band_table(wave_rows, length, band_edges):
    wave_cols = jnp.arange(length, dtype=jnp.int32)
    folded = jnp.where(wave_cols < length // 2, wave_cols, wave_cols - length)
    radius_squared = (
        wave_rows[:, None] * wave_rows[:, None] + folded[None, :] * folded[None, :]
    ).reshape(-1)
    edge_squared = band_edges * band_edges
    inside = (radius_squared[:, None] >= edge_squared[None, :-1]) & (
        radius_squared[:, None] < edge_squared[None, 1:]
    )
    return inside.astype(jnp.bfloat16)


def mode_counts(band_edges, length):
    halfway = length // 2
    wave_rows = jnp.arange(halfway, dtype=jnp.int32)
    wave_abs = jnp.arange(halfway + 1, dtype=jnp.int32)
    weights = jnp.where((wave_abs == 0) | (wave_abs == halfway), 1, 2).astype(jnp.int32)
    radius_squared = wave_rows[:, None] * wave_rows[:, None] + wave_abs[None, :] * wave_abs[None, :]

    def below_edge(edge_value):
        return jnp.sum(jnp.where(radius_squared < edge_value * edge_value, weights[None, :], 0))

    totals = lax.map(below_edge, band_edges)
    return (totals[1:] - totals[:-1]).astype(jnp.float32)


def band_partials(real_part, imag_part, first_bin, second_bin, row_start, band_edges, length):
    count_items = real_part.shape[0]
    row_count = real_part.shape[2]
    pair_count = first_bin.shape[0]
    block_rows = math.gcd(row_count, max(1, 16384 // length))

    def visit_block(running, block_index):
        offset = block_index * block_rows
        real_rows = lax.dynamic_slice_in_dim(real_part, offset, block_rows, 2).astype(jnp.float32)
        imag_rows = lax.dynamic_slice_in_dim(imag_part, offset, block_rows, 2).astype(jnp.float32)
        cross_terms = jnp.take(real_rows, first_bin, axis=1) * jnp.take(
            real_rows, second_bin, axis=1
        ) + jnp.take(imag_rows, first_bin, axis=1) * jnp.take(imag_rows, second_bin, axis=1)
        flat_terms = cross_terms.reshape(count_items * pair_count, block_rows * length)
        upper_part = flat_terms.astype(jnp.bfloat16)
        lower_part = (flat_terms - upper_part.astype(jnp.float32)).astype(jnp.bfloat16)
        wave_rows = row_start + offset + jnp.arange(block_rows, dtype=jnp.int32)
        indicator = band_table(wave_rows, length, band_edges)
        summed = jnp.dot(upper_part, indicator, preferred_element_type=jnp.float32) + jnp.dot(
            lower_part, indicator, preferred_element_type=jnp.float32
        )
        return (running + summed.reshape(count_items, pair_count, -1), None)

    initial = jnp.zeros((count_items, pair_count, band_edges.shape[0] - 1), jnp.float32)
    totals, unused = lax.scan(
        visit_block, initial, jnp.arange(row_count // block_rows, dtype=jnp.int32)
    )
    return totals


def per_device(
    density_maps, margin_src, margin_row, margin_count, class_id, coupling_bank, band_edges
):
    highest = lax.Precision.HIGHEST
    patch_local, bins_local, length, columns = density_maps.shape
    freq_count = lax.axis_size("freq")
    zbin_count = lax.axis_size("zbin")
    bins_total = bins_local * zbin_count
    patch_total = margin_src.shape[0]
    first_patch = lax.axis_index("patch") * patch_local
    column_start = lax.axis_index("freq") * columns
    edge_strips = jnp.stack(
        [density_maps[:, :, :W, :], density_maps[:, :, length - W :, :]], axis=1
    )
    nearby = extended(edge_strips, (("patch", 0),), patch_local)
    image = density_maps.astype(jnp.float32)
    patch_now = first_patch + 0
    patch_image = image[0]
    for entry_index in range(KMAX):
        strip_id = margin_src[patch_now, entry_index]
        source = strip_id // 2
        strip_side = strip_id % 2
        halo_slot = (source - first_patch + patch_local + patch_total) % patch_total
        live = (entry_index < margin_count[patch_now]).astype(jnp.float32)
        chosen = nearby[halo_slot, strip_side].astype(jnp.float32) * live
        row_at = margin_row[patch_now, entry_index]
        anchor = (jnp.int32(0), row_at, jnp.int32(0))
        current = lax.dynamic_slice(patch_image, anchor, (bins_local, W, columns))
        patch_image = lax.dynamic_update_slice(patch_image, current + chosen, anchor)
    image = image.at[0].set(patch_image)
    profile = taper_profile(length, APOD)
    column_taper = lax.dynamic_slice_in_dim(profile, column_start, columns, 0)
    tapered = (image * profile[None, None, :, None] * column_taper[None, None, None, :]).astype(
        jnp.bfloat16
    )
    pixel_index = jnp.arange(length, dtype=jnp.int32)
    cos_rows, sin_rows = fourier_tables(
        jnp.arange(length // 2, dtype=jnp.int32), pixel_index, length
    )
    cols_real = jnp.einsum(
        "ky,pbyx->pbkx", cos_rows, tapered, preferred_element_type=jnp.float32
    ).astype(jnp.bfloat16)
    cols_imag = (
        -jnp.einsum("ky,pbyx->pbkx", sin_rows, tapered, preferred_element_type=jnp.float32)
    ).astype(jnp.bfloat16)
    cos_full, sin_full = fourier_tables(pixel_index, pixel_index, length)
    joined = jnp.concatenate([cos_full, sin_full], axis=1)
    first_np, second_np = np.triu_indices(bins_total)
    first_all = jnp.asarray(first_np, dtype=jnp.int32)
    second_all = jnp.asarray(second_np, dtype=jnp.int32)
    rows_freq = length // 2 // freq_count
    row_base = lax.axis_index("freq") * rows_freq
    real_in = lax.all_to_all(cols_real, "freq", split_axis=2, concat_axis=3, tiled=True)
    imag_in = lax.all_to_all(cols_imag, "freq", split_axis=2, concat_axis=3, tiled=True)
    from_real = jnp.einsum("pbkx,xf->pbkf", real_in, joined, preferred_element_type=jnp.float32)
    from_imag = jnp.einsum("pbkx,xf->pbkf", imag_in, joined, preferred_element_type=jnp.float32)
    real_out = from_real[..., :length] + from_imag[..., length:]
    imag_out = from_imag[..., :length] - from_real[..., length:]
    modes_real = real_out.astype(jnp.bfloat16)
    modes_imag = imag_out.astype(jnp.bfloat16)
    row_start = row_base + lax.axis_index("zbin") * (rows_freq // zbin_count)
    partial_value = band_partials(
        lax.all_to_all(modes_real, "zbin", split_axis=2, concat_axis=1, tiled=True),
        lax.all_to_all(modes_imag, "zbin", split_axis=2, concat_axis=1, tiled=True),
        first_all,
        second_all,
        row_start,
        band_edges,
        length,
    )
    own_share = lax.psum_scatter(partial_value, "zbin", scatter_dimension=1, tiled=True)
    totals = lax.psum(own_share, "freq")
    counts = mode_counts(band_edges, length)
    pseudo = totals / (counts * float(length * length))[None, None, :]
    own_rows = lax.dynamic_slice_in_dim(class_id, first_patch, patch_local, 0)
    bank_piece = lax.all_gather(coupling_bank, "patch", axis=0, tiled=True)
    selector = (
        own_rows[:, None] == jnp.arange(bank_piece.shape[0], dtype=jnp.int32)[None, :]
    ).astype(jnp.float32)
    matrices = jnp.einsum("pn,nab->pab", selector, bank_piece, precision=highest)
    return jnp.zeros_like(pseudo) + jnp.einsum("pqb,pab->pqa", pseudo, matrices, precision=highest)


def solution(mesh):
    in_specs = (
        P(("groups", "patch"), "zbin", None, "freq"),
        P("groups", None),
        P("groups", None),
        P("groups"),
        P("groups"),
        P("patch", None, None),
        P(),
    )
    out_specs = P(("groups", "patch"), "zbin", None)
    return jax.shard_map(
        per_device, mesh=mesh, in_specs=in_specs, out_specs=out_specs, check_vma=False
    )
```

profile of v0, /device:TPU:0, one launch (start us, length us, event | category | flops | bytes accessed | tf_op | source)
XLA Modules:
  0.0 720.3 jit_solution(13449480150437806697)
XLA Ops:
  0.9 3.1 collective-permute-start
  4.0 2.1 collective-permute-start.1
  6.1 6.0 fusion.68
  12.2 17.6 %sine_convert_fusion = (bf16[1024,1024]{1,0:T(8,128)(2,1)S(1)}, bf16[1024,1024]{1,0:T(8,128)(2,1)}) fusion(), kind=kLoop, calls=%fused_computation.46 | loop fusion | flops 16777216 | bytes 4194304 | tf_op jit(solution)/shard_map/convert_element_type | solution.py:40
  52.4 1.7 dynamic_update_slice.19
  55.0 1.7 dynamic_update_slice.20
  57.6 1.7 dynamic_update_slice.21
  60.2 2.2 dynamic_update_slice.22
  62.4 12.1 %fusion.38 = bf16[1,2,512,512]{2,3,1,0:T(8,128)(2,1)} fusion(f32[1,2,1024,512]{3,2,1,0:T(8,128)} %dynamic_update_slice.22, f32[512]{0:T(512)S(1)} %dynamic_slice.103, f32[1024]{0:T(1024)S(1)} %subtract_select_fusion), kind=kOutput, calls=%fused_computation.73 | convolution fusion | flops 1085800448 | bytes 5249024 | tf_op jit(solution)/shard_map/ky,pbyx->pbkx/dot_general | solution.py:143
  74.5 9.8 %fusion.37 = bf16[1,2,512,512]{2,3,1,0:T(8,128)(2,1)} fusion(f32[1,2,1024,512]{3,2,1,0:T(8,128)S(1)} %copy-done, f32[512]{0:T(512)S(1)} %dynamic_slice.103, f32[1024]{0:T(1024)S(1)} %subtract_select_fusion), kind=kOutput, calls=%fused_computation.72 | convolution fusion | flops 1085276160 | bytes 5249024 | tf_op jit(solution)/shard_map/ky,pbyx->pbkx/dot_general | solution.py:139
  84.3 2.5 copy.33
  86.9 4.6 all_to_all.66
  91.4 1.1 copy.56
  92.5 1.6 reshape.214
  94.1 2.5 copy.30
  96.6 4.8 all_to_all.67
  101.4 1.1 copy.57
  102.4 1.6 reshape.213
  104.0 4.4 convolution_bitcast_fusion
  108.4 2.3 convolution_bitcast_fusion.1
  110.8 1.2 fusion.32
  112.0 2.1 copy.35
  114.1 3.6 all-to-all-start.2
  117.7 470.5 %while.26 = (s32[]{:T(128)}, s32[129]{0:T(256)S(1)}, s32[129]{0:T(256)S(1)}, s32[513]{0:T(1024)S(1)}, s32[512]{0:T(512)S(1)}, /*index=5*/s32[]{:T(128)}) while((s32[]{:T(128)}, s32[129]{0:T(256)S(1)}, s32[129]{0:T(256)S(1)}, s32[513]{0:T(1024)S(1)}, s32[512]{0:T(512)S(1)}, /*index=5*/s32[]{:T(128)}) %tuple.85), condition=%wide.region_6.8_spmd.clone, body=%wide.region_4.7_spmd.clone.sunk | while | flops 1052678 | bytes 8317 | solution.py:66
  119.6 1.0 select_reduce_fusion.2
  123.2 1.0 select_reduce_fusion.2
  126.9 1.0 select_reduce_fusion.2
  130.5 1.0 select_reduce_fusion.2
  137.8 1.0 select_reduce_fusion.2
  141.5 1.0 select_reduce_fusion.2
  145.1 1.0 select_reduce_fusion.2
  590.1 2.0 copy.37
  592.1 3.6 all-to-all-start.3
  595.7 13.9 %all_gather.3 = f32[4,128,128]{2,1,0:T(8,128)S(1)} all-gather(f32[1,128,128]{2,1,0:T(8,128)S(1)} %copy-done.5), channel_id=1, replica_groups=mesh['groups'=2,'patch'=4,'zbin'=2,'freq'=2] {'patch'}, dimensions={0}, use_global_device_ids=true | all-gather | bytes 327680 | tf_op jit(solution)/shard_map/all_gather | solution.py:175
  610.2 1.8 fusion.45
  612.3 1.3 copy.38
  614.1 95.5 %while.27 = (s32[]{:T(128)}, f32[1,10,128]{2,1,0:T(8,128)}, s32[8]{0:T(128)}, bf16[1,4,128,1024]{3,2,1,0:T(8,128)(2,1)S(1)}, bf16[1,4,128,1024]{3,2,1,0:T(8,128)...) while((s32[]{:T(128)}, f32[1,10,128]{2,1,0:T(8,128)}, ...), condition=%wide.region_1.3_spmd.clone.clone, body=%wide.region_0.2_spmd.sunk.clone.clone.sunk | while | flops 97937192 | bytes 23216832 | solution.py:94
  614.4 1.4 dynamic_slice.138
  621.0 2.3 fusion.84
  623.4 2.4 fusion.85
  626.3 1.3 dynamic_slice.138
  632.9 2.3 fusion.84
  635.2 2.4 fusion.85
  638.2 1.3 dynamic_slice.138
  644.8 2.3 fusion.84
  647.1 2.4 fusion.85
  650.1 1.3 dynamic_slice.138
  656.7 2.3 fusion.84
  659.0 2.4 fusion.85
  662.0 1.3 dynamic_slice.138
  668.6 2.3 fusion.84
  670.9 2.4 fusion.85
  673.9 1.3 dynamic_slice.138
  680.5 2.3 fusion.84
  682.8 2.4 fusion.85
  685.8 1.3 dynamic_slice.138
  692.4 2.3 fusion.84
  694.7 2.4 fusion.85
  697.7 1.3 dynamic_slice.138
  704.3 2.3 fusion.84
  706.6 2.4 fusion.85
  710.3 5.0 all-reduce
  715.3 2.5 psum.7
  718.4 1.0 convolution_bitcast_fusion.2
  (746 shorter events, 346.6 us)
Async XLA Ops:
  0.9 50.4 %collective-permute-start = (bf16[1,2,2,32,512]{4,3,2,1,0:T(8,128)(2,1)S(1)}, bf16[1,2,2,32,512]{4,3,2,1,0:T(8,128)(2,1)S(1)}, u32[]{:S(2)}, u32[]{:S(2)}) collective-permute-start(bf16[1,2,2,32,512]{4,3,2,1,0:T(8,128)(2,1)S(1)} %pad_maximum_fusion.1), channel_id=1, source_target_pairs={{0,4},{4,8},{8,12},{12,0},{1,5},{5,9},{9,13},{13,1},{2,6},{6,10},{... | collective-permute-start | bytes 393224 | tf_op jit(solution)/shard_map/ppermute | solution.py:21
  4.0 47.4 %collective-permute-start.1 = (bf16[1,2,2,32,512]{4,3,2,1,0:T(8,128)(2,1)S(1)}, bf16[1,2,2,32,512]{4,3,2,1,0:T(8,128)(2,1)S(1)}, u32[]{:S(2)}, u32[]{:S(2)}) collective-permute-start(bf16[1,2,2,32,512]{4,3,2,1,0:T(8,128)(2,1)S(1)} %pad_maximum_fusion.1), channel_id=1, source_target_pairs={{4,0},{8,4},{12,8},{0,12},{5,1},{9,5},{13,9},{1,13},{6,2},{10,6},{... | collective-permute-start | bytes 393224 | tf_op jit(solution)/shard_map/ppermute | solution.py:23
  12.1 17.7 %copy-start.11 = (s32[4,4]{1,0:T(4,128)S(1)}, s32[4,4]{1,0:T(4,128)}, u32[]{:S(2)}) copy-start(s32[4,4]{1,0:T(4,128)} %param.18) | copy-start | bytes 196
  12.1 17.7 %copy-start.12 = (s32[4,4]{1,0:T(4,128)S(1)}, s32[4,4]{1,0:T(4,128)}, u32[]{:S(2)}) copy-start(s32[4,4]{1,0:T(4,128)} %param.19) | copy-start | bytes 196
  12.2 33.2 %copy-start.13 = (s32[4]{0:T(128)S(1)}, s32[4]{0:T(128)}, u32[]{:S(2)}) copy-start(s32[4]{0:T(128)} %param.20) | copy-start | bytes 52
  62.4 12.1 %copy-start = (f32[1,2,1024,512]{3,2,1,0:T(8,128)S(1)}, f32[1,2,1024,512]{3,2,1,0:T(8,128)}, u32[]{:S(2)}) copy-start(f32[1,2,1024,512]{3,2,1,0:T(8,128)} %dynamic_update_slice.22) | copy-start | bytes 12582916
  104.0 4.4 copy-start.3
  104.0 4.4 copy-start.4
  112.0 5.7 copy-start.10
  112.0 476.2 %copy-start.14 = (s32[4]{0:T(128)S(1)}, s32[4]{0:T(128)}, u32[]{:S(2)}) copy-start(s32[4]{0:T(128)} %param.21) | copy-start | bytes 52
  112.0 476.8 %copy-start.15 = (u32[32]{0:T(128)S(1)}, u32[32]{0:T(128)}, u32[]{:S(2)}) copy-start(u32[32]{0:T(128)} %constant.287) | copy-start | bytes 388
  114.1 478.0 %all-to-all-start.2 = ((bf16[1,2,256,1024]{3,1,0,2:T(2,128)(2,1)}), bf16[1,2,256,1024]{3,1,0,2:T(2,128)(2,1)S(1)}, u32[]{:S(2)}, u32[]{:S(2)}) async-start(bf16[1,2,256,1024]{3,1,0,2:T(2,128)(2,1)} %copy.35), calls=%async_computation.2 | async-start | bytes 2097152 | tf_op jit(solution)/shard_map/all_to_all | solution.py:162
  590.0 5.7 copy-start.5
  592.1 20.2 %all-to-all-start.3 = ((bf16[1,2,256,1024]{3,1,0,2:T(2,128)(2,1)}), bf16[1,2,256,1024]{3,1,0,2:T(2,128)(2,1)S(1)}, u32[]{:S(2)}, u32[]{:S(2)}) async-start(bf16[1,2,256,1024]{3,1,0,2:T(2,128)(2,1)} %copy.37), calls=%async_computation.3 | async-start | bytes 2097152 | tf_op jit(solution)/shard_map/all_to_all | solution.py:163
  612.0 2.1 copy-start.6
  612.0 2.1 copy-start.7
  614.4 4.3 copy-start.1
  621.0 2.3 copy-start.8
  623.3 3.0 copy-start.2
  625.7 0.6 copy-start.9
  626.3 4.2 copy-start.1
  632.9 2.3 copy-start.8
  635.2 3.0 copy-start.2
  637.6 0.6 copy-start.9
  638.2 4.2 copy-start.1
  644.8 2.3 copy-start.8
  647.1 3.0 copy-start.2
  649.5 0.6 copy-start.9
  650.1 4.2 copy-start.1
  656.7 2.3 copy-start.8
  659.0 3.0 copy-start.2
  661.4 0.6 copy-start.9
  662.0 4.2 copy-start.1
  668.6 2.3 copy-start.8
  670.9 3.0 copy-start.2
  673.3 0.6 copy-start.9
  673.9 4.2 copy-start.1
  680.5 2.3 copy-start.8
  682.8 3.0 copy-start.2
  685.2 0.6 copy-start.9
  685.8 4.2 copy-start.1
  692.4 2.3 copy-start.8
  694.7 3.0 copy-start.2
  697.1 0.6 copy-start.9
  697.7 4.2 copy-start.1
  704.3 2.3 copy-start.8
  706.6 3.0 copy-start.2
  709.0 0.6 copy-start.9
where the time goes:
time: 731 us; the launch traced here: 720 us
  local copies, waits for them, and re-layouts  245 us (34%)
  loops' own time  175 us (24%)
  other arithmetic  166 us (23%)
  matrix products  69 us (9%)
  blocking collectives  30.7 us (4%)
  between operations  21.3 us (3%)
  starting transfers between devices  12.3 us (2%)
    another operation x1, loops' own time, mode_counts(): totals = lax.map(below_edge, band_edges)  168 us
    reduce_sum x129, other arithmetic, below_edge(): jnp.sum(jnp.where(radius_squared < edge_value * edge_value, weights[None,...  126 us
    dynamic_update_slice x129, local copies, waits for them, and re-layouts, mode_counts(): totals = lax.map(below_edge, band_edges)  101 us
    dynamic_slice x129, local copies, waits for them, and re-layouts, mode_counts(): totals = lax.map(below_edge, band_edges)  75.2 us
    dot_general x8, matrix products, visit_block(): jnp.dot(upper_part, indicator, preferred_element_type=jnp.float32)  18.8 us
    dot_general x8, matrix products, visit_block(): jnp.dot(lower_part, indicator, preferred_element_type=jnp.float32)  18.7 us
    convert_element_type x1, other arithmetic, fourier_tables(): jnp.sin(angles).astype(jnp.bfloat16)  17.6 us
  transfers between devices with their start and end apart: 4, of which 0 were waited for; matrix products, arithmetic and copies ran while one was open for 46% of the time, Pallas kernels for 0%

commit v1 on v0

v1 whole, which is shorter than its diff:
```python
import math

import jax
import jax.numpy as jnp
import ml_dtypes
import numpy as np
from jax import lax
from jax.experimental import pallas as pl
from jax.experimental.pallas import tpu as pltpu
from jax.sharding import PartitionSpec as P

W = 32
APOD = 64
LANES = 128
VMEM = pl.BlockSpec(memory_space=pltpu.VMEM)
PARAMS = dict(vmem_limit_bytes=48 * 1024 * 1024)


def taper_profile(length, ramp_width):
    position = np.arange(length)
    distance = np.minimum(position, length - 1 - position)
    ramped = 0.5 - 0.5 * np.cos(math.pi * (distance + 0.5) / ramp_width)
    return np.where(distance < ramp_width, ramped, 1.0).astype(np.float32)


def fourier_tables(length):
    half = length // 2
    phases = np.arange(half)[:, None] * np.arange(length)[None, :] % length
    angles = phases * (2.0 * math.pi / length)
    return (
        np.cos(angles).astype(np.float32).astype(ml_dtypes.bfloat16),
        np.sin(angles).astype(np.float32).astype(ml_dtypes.bfloat16),
    )


def edge_reach(edge_squared, wave_rows):
    room = edge_squared - wave_rows * wave_rows
    reach = jnp.sqrt(jnp.maximum(room, 0).astype(jnp.float32)).astype(jnp.int32) - 1
    for _ in range(3):
        reach = reach + (reach * reach < room).astype(jnp.int32)
    return jnp.where(room > 0, reach, 0)


def first_kernel(maps_ref, strips_ref, pick_ref, row_taper_ref, col_taper_ref, table_ref, out_ref, tapered):
    bins, length, columns = maps_ref.shape
    block = 256

    @pl.when(pl.program_id(0) == 0)
    def _():
        for b in range(bins):
            for r in range(0, length, block):
                rows = pl.ds(r, block)
                image = maps_ref[b, rows, :].astype(jnp.float32) + jnp.dot(
                    pick_ref[rows, :], strips_ref[b], preferred_element_type=jnp.float32
                )
                tapered[b, rows, :] = (image * row_taper_ref[rows, :] * col_taper_ref[...]).astype(jnp.bfloat16)

    for b in range(bins):
        out_ref[0, 0, b] = jnp.dot(table_ref[...], tapered[b], preferred_element_type=jnp.float32).astype(jnp.bfloat16)


def second_kernel(cols_ref, cos_ref, sin_ref, out_ref):
    sources, _, _, _, columns = cols_ref.shape

    def product(part, table_ref):
        total = None
        for s in range(sources):
            term = jnp.dot(
                cols_ref[s, part, 0],
                table_ref[pl.ds(s * columns, columns), :],
                preferred_element_type=jnp.float32,
            )
            total = term if total is None else total + term
        return total

    real_cos, imag_sin = product(0, cos_ref), product(1, sin_ref)
    out_ref[0, 0, 0] = (real_cos + imag_sin).astype(jnp.bfloat16)
    out_ref[0, 0, 1] = (real_cos - imag_sin).astype(jnp.bfloat16)
    imag_cos, real_sin = product(1, cos_ref), product(0, sin_ref)
    out_ref[0, 0, 2] = (imag_cos - real_sin).astype(jnp.bfloat16)
    out_ref[0, 0, 3] = (imag_cos + real_sin).astype(jnp.bfloat16)


def band_kernel(pairs, modes_ref, row_ref, edges_ref, low_ref, prefix_ref, out_ref):
    _, local, _, rows, half = modes_ref.shape
    wave_rows = row_ref[0, 0] + lax.broadcasted_iota(jnp.int32, (rows, LANES), 0)
    lane = lax.broadcasted_iota(jnp.int32, (rows, LANES), 1)
    edges = edges_ref[...]
    reach = edge_reach(edges * edges, wave_rows)
    low = low_ref[0, 0]
    weight = jnp.where(lane == 0, 0.5, 1.0)
    prefix = prefix_ref[...]
    out_ref[...] = jnp.zeros_like(out_ref)
    for b in range(half // LANES):
        columns = pl.ds(b * LANES, LANES)
        index = jnp.clip(reach - b * LANES, 1, LANES) - 1
        inside = reach > b * LANES
        wave_cols = lane + b * LANES
        scale = (wave_rows * wave_rows + wave_cols * wave_cols >= low * low).astype(jnp.float32)
        if b == 0:
            scale = scale * weight
        for n, (i, j) in enumerate(pairs):
            cross = None
            for c in range(4):
                term = modes_ref[i // local, i % local, c, :, columns].astype(jnp.float32) * modes_ref[
                    j // local, j % local, c, :, columns
                ].astype(jnp.float32)
                cross = term if cross is None else cross + term
            cross = cross * scale
            upper = cross.astype(jnp.bfloat16)
            lower = (cross - upper.astype(jnp.float32)).astype(jnp.bfloat16)
            sums = jnp.dot(
                jnp.concatenate([upper, lower], axis=1), prefix, preferred_element_type=jnp.float32
            )
            taken = jnp.where(inside, jnp.take_along_axis(sums, index, axis=1), 0.0)
            out_ref[pl.ds(n, 1), :] += jnp.sum(taken, axis=0, keepdims=True)


def per_device(density_maps, margin_src, margin_row, margin_count, class_id, coupling_bank, band_edges):
    _, bins_local, length, columns = density_maps.shape
    half = length // 2
    freq_count = lax.axis_size("freq")
    zbin_count = lax.axis_size("zbin")
    patch_count = lax.axis_size("patch")
    bins_total = bins_local * zbin_count
    me = lax.axis_index("patch")
    rows_freq = half // freq_count
    rows_zbin = rows_freq // zbin_count

    maps = density_maps[0]
    strips = jnp.concatenate([maps[:, :W, :], maps[:, length - W :, :]], axis=1)
    from_left = lax.ppermute(strips, "patch", [(i, (i + 1) % patch_count) for i in range(patch_count)])
    from_right = lax.ppermute(strips, "patch", [((i + 1) % patch_count, i) for i in range(patch_count)])
    nearby = jnp.concatenate([from_left, from_right], axis=1)

    source = margin_src[me]
    side = jnp.where(source // 2 == (me + patch_count - 1) % patch_count, 0, 1)
    slot = (side * 2 + source % 2) * W
    live = jnp.arange(source.shape[0]) < margin_count[me]
    pixel = jnp.arange(length, dtype=jnp.int32)[:, None, None]
    place = jnp.arange(4 * W, dtype=jnp.int32)[None, :, None]
    strip_row = place - slot[None, None, :]
    hit = (strip_row >= 0) & (strip_row < W) & (pixel == margin_row[me][None, None, :] + strip_row) & live[None, None, :]
    pick = jnp.sum(hit.astype(jnp.float32), axis=2).astype(jnp.bfloat16)

    profile = taper_profile(length, APOD)
    col_taper = lax.dynamic_slice_in_dim(jnp.asarray(profile), lax.axis_index("freq") * columns, columns, 0)
    cos_np, sin_np = fourier_tables(length)
    minus_sin = (-sin_np.astype(np.float32)).astype(ml_dtypes.bfloat16)
    table = jnp.asarray(np.concatenate([cos_np, minus_sin], axis=0))
    cols = pl.pallas_call(
        first_kernel,
        grid=(2 * freq_count,),
        out_shape=jax.ShapeDtypeStruct((freq_count, 2, bins_local, rows_freq, columns), jnp.bfloat16),
        in_specs=[VMEM] * 5 + [pl.BlockSpec((rows_freq, length), lambda i: (i, 0))],
        out_specs=pl.BlockSpec(
            (1, 1, bins_local, rows_freq, columns), lambda i: (i % freq_count, i // freq_count, 0, 0, 0)
        ),
        scratch_shapes=[pltpu.VMEM((bins_local, length, columns), jnp.bfloat16)],
        compiler_params=pltpu.CompilerParams(**PARAMS),
        name="first_transform",
    )(maps, nearby, pick, jnp.asarray(profile)[:, None], col_taper[None, :], table)

    cols = lax.all_to_all(cols, "freq", split_axis=0, concat_axis=0, tiled=True)

    modes = pl.pallas_call(
        second_kernel,
        grid=(zbin_count, bins_local),
        out_shape=jax.ShapeDtypeStruct((zbin_count, bins_local, 4, rows_zbin, half), jnp.bfloat16),
        in_specs=[
            pl.BlockSpec((freq_count, 2, 1, rows_zbin, columns), lambda z, b: (0, 0, b, z, 0)),
            VMEM,
            VMEM,
        ],
        out_specs=pl.BlockSpec((1, 1, 4, rows_zbin, half), lambda z, b: (z, b, 0, 0, 0)),
        compiler_params=pltpu.CompilerParams(**PARAMS),
        name="second_transform",
    )(cols, jnp.asarray(np.ascontiguousarray(cos_np.T)), jnp.asarray(np.ascontiguousarray(sin_np.T)))

    modes = lax.all_to_all(modes, "zbin", split_axis=0, concat_axis=0, tiled=True)

    first_np, second_np = np.triu_indices(bins_total)
    pairs = [(int(i), int(j)) for i, j in zip(first_np, second_np)]
    row_start = lax.axis_index("freq") * rows_freq + lax.axis_index("zbin") * rows_zbin
    ones = np.triu(np.ones((LANES, LANES)))
    prefix = jnp.asarray(np.concatenate([ones, ones], axis=0).astype(ml_dtypes.bfloat16))
    smem = pl.BlockSpec(memory_space=pltpu.SMEM)
    discs = pl.pallas_call(
        lambda *refs: band_kernel(pairs, *refs),
        out_shape=jax.ShapeDtypeStruct((len(pairs), LANES), jnp.float32),
        in_specs=[VMEM, smem, VMEM, smem, VMEM],
        out_specs=VMEM,
        compiler_params=pltpu.CompilerParams(**PARAMS),
        name="band_sums",
    )(modes, row_start.reshape(1, 1), band_edges[None, 1:], band_edges[:1].reshape(1, 1), prefix)

    share = lax.psum_scatter(discs, "zbin", scatter_dimension=0, tiled=True)
    share = lax.psum(share, "freq")
    totals = share - jnp.pad(share, ((0, 0), (1, 0)))[:, :-1]

    reach = edge_reach(
        (band_edges * band_edges)[None, :], jnp.arange(half, dtype=jnp.int32)[:, None]
    )
    below = jnp.sum(jnp.maximum(2 * reach - 1, 0), axis=0)
    counts = (below[1:] - below[:-1]).astype(jnp.float32)
    pseudo = totals / (counts * float(length * length))[None, :]
    bank = lax.all_gather(coupling_bank, "patch", axis=0, tiled=True)
    matrix = lax.dynamic_index_in_dim(bank, class_id[me], 0, keepdims=False)
    return jnp.einsum("qb,ab->qa", pseudo, matrix, precision=lax.Precision.HIGHEST)[None]


def solution(mesh):
    in_specs = (
        P(("groups", "patch"), "zbin", None, "freq"),
        P("groups", None),
        P("groups", None),
        P("groups"),
        P("groups"),
        P("patch", None, None),
        P(),
    )
    out_specs = P(("groups", "patch"), "zbin", None)
    return jax.shard_map(
        per_device, mesh=mesh, in_specs=in_specs, out_specs=out_specs, check_vma=False
    )
```

time: 731 us -> 72.8 us (0.10); the launches traced: 720 us -> 72.1 us
  local copies, waits for them, and re-layouts: 245 us -> 7.97 us
  loops' own time: 175 us -> 0 us
  other arithmetic: 166 us -> 2.57 us
  matrix products: 69 us -> 0.21 us
  between operations: 21.3 us -> 2.65 us
  Pallas kernels: 0 us -> 13.5 us
  waiting for transfers between devices: 0.01 us -> 8.36 us
    another operation x2 -> x0, loops' own time: 175 us -> none  [the longest x1 168 us: mode_counts(): totals = lax.map(below_edge, band_edges)]
    reduce_sum x129 -> x2, other arithmetic: 126 us -> 0.96 us  [the longest x1 0.5 us: per_device(): pick = jnp.sum(hit.astype(jnp.float32), axis=2).astype(jnp.bfloat16)]
    dynamic_update_slice x133 -> x0, local copies, waits for them, and re-layouts: 108 us -> none  [the longest x129 101 us: mode_counts(): totals = lax.map(below_edge, band_edges)]
    dynamic_slice x141 -> x4, local copies, waits for them, and re-layouts: 87.7 us -> 2.6 us  [the longest x1 1.24 us: per_device(): live = jnp.arange(source.shape[0]) < margin_count[me]]
    dot_general x22 -> x1, matrix products: 69 us -> 0.21 us  [per_device(): jnp.einsum('qb,ab->qa', pseudo, matrix, precision=lax.Precision.HIGHEST)]
    convert_element_type x3 -> x0, other arithmetic: 24.8 us -> none  [the longest x1 17.6 us: fourier_tables(): jnp.sin(angles).astype(jnp.bfloat16)]
    gather x32 -> x0, local copies, waits for them, and re-layouts: 18.9 us -> none  [the longest x8 4.72 us: visit_block(): jnp.take(imag_rows, second_bin, axis=1)]
    pallas_call x0 -> x3, Pallas kernels: none -> 13.5 us  [the longest x1 5.33 us: per_device(): pl.pallas_call(second_kernel, grid=(zbin_count, bins_local), out_shape=ja...]
  transfers between devices with their start and end apart: 4 -> 3, of which waited for: 0 -> 3; matrix products, arithmetic and copies ran while one was open for 46% -> 9% of each run, Pallas kernels for 0% -> 0%
where the time goes in v1:
time: 72.8 us; the launch traced here: 72.1 us
  blocking collectives  27.7 us (38%)
  Pallas kernels  13.5 us (19%)
  starting transfers between devices  9.07 us (12%)
  waiting for transfers between devices  8.36 us (11%)
  local copies, waits for them, and re-layouts  7.97 us (11%)
  between operations  2.65 us (4%)
  other arithmetic  2.57 us (4%)
    all_gather x1, blocking collectives, per_device(): bank = lax.all_gather(coupling_bank, 'patch', axis=0, tiled=True)  13.8 us
    all_to_all x1, waiting for transfers between devices, per_device(): lax.all_to_all(modes, 'zbin', split_axis=0, concat_axis=0, tiled=True)  6.71 us
    all_to_all x1, blocking collectives, per_device(): cols = lax.all_to_all(cols, 'freq', split_axis=0, concat_axis=0, tiled=True)  6.45 us
    pallas_call x1, Pallas kernels, per_device(): pl.pallas_call(second_kernel, grid=(zbin_count, bins_local), out_shape=ja...  5.33 us
    pallas_call x1, Pallas kernels, per_device(): pl.pallas_call(first_kernel, grid=(2 * freq_count,), out_shape=jax.ShapeD...  5.07 us
    unnamed x1, blocking collectives  5.01 us
    all_to_all x1, starting transfers between devices, per_device(): lax.all_to_all(modes, 'zbin', split_axis=0, concat_axis=0, tiled=True)  3.91 us
    unnamed x22, local copies, waits for them, and re-layouts  3.25 us
  transfers between devices with their start and end apart: 3, of which 3 were waited for; matrix products, arithmetic and copies ran while one was open for 9% of the time, Pallas kernels for 0%

profile of v1, /device:TPU:0, one launch (start us, length us, event | category | flops | bytes accessed | tf_op | source)
XLA Modules:
  0.0 72.1 jit_solution(17107923586204083484)
XLA Ops:
  0.0 0.0 copy-start
  0.0 0.9 %fusion.25 = (bf16[2,32,512]{2,1,0:T(8,128)(2,1)S(1)}, bf16[2,32,512]{2,1,0:T(8,128)(2,1)S(1)}) fusion(bf16[2,1024,512]{2,1,0:T(8,128)(2,1)} %bitcast.22), kind=kLoop, calls=%fused_computation.50 | loop fusion | bytes 262144 | tf_op jit(solution)/shard_map/slice | solution.py:131
  0.9 3.1 %collective-permute-start = (bf16[2,64,512]{2,1,0:T(8,128)(2,1)S(1)}, bf16[2,64,512]{2,1,0:T(8,128)(2,1)S(1)}, u32[]{:S(2)}, u32[]{:S(2)}) collective-permute-start(bf16[2,64,512]{2,1,0:T(8,128)(2,1)S(1)} %pad_maximum_fusion.1), channel_id=1, source_target_pairs={{0,4},{4,8},{8,12},{12,0},{1,5},{5,9},{9,13},{13,1},{2,6},{6,10},{... | collective-permute-start | bytes 393224 | tf_op jit(solution)/shard_map/ppermute | solution.py:132
  4.0 2.1 %collective-permute-start.1 = (bf16[2,64,512]{2,1,0:T(8,128)(2,1)S(1)}, bf16[2,64,512]{2,1,0:T(8,128)(2,1)S(1)}, u32[]{:S(2)}, u32[]{:S(2)}) collective-permute-start(bf16[2,64,512]{2,1,0:T(8,128)(2,1)S(1)} %pad_maximum_fusion.1), channel_id=1, source_target_pairs={{4,0},{8,4},{12,8},{0,12},{5,1},{9,5},{13,9},{1,13},{6,2},{10,6},{... | collective-permute-start | bytes 393224 | tf_op jit(solution)/shard_map/ppermute | solution.py:133
  6.1 0.0 copy-done
  6.1 0.7 fusion.23
  6.8 0.1 fusion.17
  6.9 0.1 fusion.14
  6.9 1.2 %dynamic_slice.24 = s32[1]{0:T(128)} dynamic-slice(s32[4]{0:T(128)} %param.15, s32[]{:T(128)S(6)} %select_n.51), dynamic_slice_sizes={1} | dynamic-slice | bytes 12 | tf_op jit(solution)/shard_map/dynamic_slice | solution.py:139
  8.2 0.6 iota_compare_fusion.1
  8.8 0.8 %dynamic_slice.25 = f32[512]{0:T(512)S(1)} dynamic-slice(f32[1024]{0:T(1024)} %constant.90.clone, s32[]{:T(128)S(6)} %select_n.56), dynamic_slice_sizes={512} | dynamic-slice | bytes 4100 | tf_op jit(solution)/shard_map/dynamic_slice | solution.py:147
  9.6 0.5 convert_reduce_fusion.pick_ref
  10.1 0.2 collective-permute-done
  10.4 1.4 %collective-permute-done.1 = bf16[2,64,512]{2,1,0:T(8,128)(2,1)S(1)} collective-permute-done((bf16[2,64,512]{2,1,0:T(8,128)(2,1)S(1)}, bf16[2,64,512]{2,1,0:T(8,128)(2,1)S(1)}, u32[]{:S(2)}, u32[]{:S(2)}) %collective-permute-start.1) | collective-permute-done | bytes 131104 | tf_op jit(solution)/shard_map/ppermute | solution.py:133
  11.8 0.0 copy-start.1
  11.8 1.6 %copy-done.1 = bf16[1,2,1024,512]{3,2,1,0:T(8,128)(2,1)S(1)} copy-done((bf16[1,2,1024,512]{3,2,1,0:T(8,128)(2,1)S(1)}, bf16[1,2,1024,512]{3,2,1,0:T(8,128)(2,1)}, u32[]{:S(2)}) %copy-start.1) | copy-done | bytes 2097176
  13.4 0.0 copy-start.4
  13.4 1.0 %copy-done.4 = f32[1024,1]{1,0:T(8,128)S(1)} copy-done((f32[1024,1]{1,0:T(8,128)S(1)}, f32[1024,1]{1,0:T(8,128)}, u32[]{:S(2)}) %copy-start.4) | copy-done | bytes 4120
  14.4 5.1 %first_transform.1 = bf16[2,2,2,256,512]{4,3,2,1,0:T(8,128)(2,1)S(1)} custom-call(bf16[2,1024,512]{2,1,0:T(8,128)(2,1)S(1)} %bitcast.23, bf16[2,128,512]{2,1,0:T(8,128)(2,1)S(1)} %pad_maximum_fusion.strips_ref, bf16[1024,128]{1,0:T(8,128)(2,1)S(1)} %convert_reduce_fusion.pick_ref, f32[1024,1]{1,0:T(8,128)S(1)} %copy-done.4, f32[1,512]{1,0:T(1,128)S(1)} %bitcast.24, ...), custom_call_target="tpu_custom_call" | custom-call | tf_op jit(solution)/shard_map/first_transform/pallas_call | solution.py:151
  19.5 0.0 copy-start.2
  19.5 0.0 copy-start.3
  19.5 6.5 %all_to_all.10.cols_ref = bf16[2,2,2,256,512]{4,3,2,1,0:T(8,128)(2,1)} all-to-all(bf16[2,2,2,256,512]{4,3,2,1,0:T(8,128)(2,1)S(1)} %first_transform.1), channel_id=1, replica_groups=mesh['groups'=2,'patch'=4,'zbin'=2,'freq'=2] {'freq'}, dimensions={0} | all-to-all | bytes 4194304 | tf_op jit(solution)/shard_map/all_to_all | solution.py:164
  26.0 0.0 copy-done.2
  26.0 0.0 copy-done.3
  26.0 5.3 %second_transform.1 = bf16[2,2,4,128,512]{4,3,2,1,0:T(8,128)(2,1)} custom-call(bf16[2,2,2,256,512]{4,3,2,1,0:T(8,128)(2,1)} %all_to_all.10.cols_ref, bf16[1024,512]{1,0:T(8,128)(2,1)S(1)} %copy-done.2, bf16[1024,512]{1,0:T(8,128)(2,1)S(1)} %copy-done.3), custom_call_target="tpu_custom_call" | custom-call | tf_op jit(solution)/shard_map/second_transform/pallas_call | solution.py:166
  31.3 0.0 copy-start.8
  31.3 0.0 copy-start.7
  31.3 0.0 copy-start.9
  31.3 0.0 copy-start.6
  31.3 0.0 copy-start.5
  31.3 3.9 %all-to-all-start.1 = ((bf16[2,2,4,128,512]{4,3,2,1,0:T(8,128)(2,1)}), bf16[2,2,4,128,512]{4,3,2,1,0:T(8,128)(2,1)S(1)}, u32[]{:S(2)}, u32[]{:S(2)}) async-start(bf16[2,2,4,128,512]{4,3,2,1,0:T(8,128)(2,1)} %second_transform.1), calls=%async_computation.1 | async-start | bytes 4194304 | tf_op jit(solution)/shard_map/all_to_all | solution.py:180
  35.3 0.0 copy-done.8
  35.3 0.6 dynamic_slice.26
  37.2 0.0 copy-done.7
  37.2 0.5 slice.24
  37.7 0.0 copy-done.9
  37.7 0.6 dynamic-slice
  39.5 0.0 copy-done.6
  39.5 13.8 %all_gather.3 = f32[4,128,128]{2,1,0:T(8,128)S(1)} all-gather(f32[1,128,128]{2,1,0:T(8,128)S(1)} %copy-done.6), channel_id=1, replica_groups=mesh['groups'=2,'patch'=4,'zbin'=2,'freq'=2] {'patch'}, dimensions={0}, use_global_device_ids=true | all-gather | bytes 327680 | tf_op jit(solution)/shard_map/all_gather | solution.py:207
  53.3 0.5 maximum_reduce_fusion
  53.8 0.1 slice_bitcast_fusion.refs_2_
  53.8 0.1 convert_multiply_fusion
  53.9 6.7 %all-to-all-done.1.refs_0_ = bf16[2,2,4,128,512]{4,3,2,1,0:T(8,128)(2,1)S(1)} async-done(((bf16[2,2,4,128,512]{4,3,2,1,0:T(8,128)(2,1)}), bf16[2,2,4,128,512]{4,3,2,1,0:T(8,128)(2,1)S(1)}, u32[]{:S(2)}, u32[]{:S(2)}) %all-to-all-start.1) | async-done | bytes 2097184 | tf_op jit(solution)/shard_map/all_to_all | solution.py:180
  60.6 0.0 copy-done.5
  60.6 3.1 %band_sums.1 = f32[10,128]{1,0:T(8,128)S(1)} custom-call(bf16[2,2,4,128,512]{4,3,2,1,0:T(8,128)(2,1)S(1)} %all-to-all-done.1.refs_0_, s32[1,1]{1,0:T(1,128)} %bitcast.5.refs_1_, s32[1,128]{1,0:T(1,128)S(1)} %slice_bitcast_fusion.refs_2_, s32[1,1]{1,0:T(1,128)} %bitcast.7.refs_3_, bf16[256,128]{1,0:T(8,128)(2,1)S(1)} %copy-done.5), custom_call_target="tpu_custom_call" | custom-call | tf_op jit(solution)/shard_map/band_sums/pallas_call | solution.py:188
  63.8 5.0 %all-reduce.1 = f32[10,128]{1,0:T(8,128)S(1)} all-reduce(f32[10,128]{1,0:T(8,128)S(1)} %band_sums.1), channel_id=2, replica_groups=mesh['groups'=2,'patch'=4,'zbin'=2,'freq'=2] {'zbin'}, use_global_device_ids=true, to_apply=%region_1.2.clone | all-reduce | flops 1280 | bytes 10240
  68.8 2.5 %psum.7 = f32[5,128]{1,0:T(8,128)S(1)} all-reduce(f32[5,128]{1,0:T(8,128)S(1)} %constant_dynamic-slice_fusion.2), channel_id=1, replica_groups=mesh['groups'=2,'patch'=4,'zbin'=2,'freq'=2] {'freq'}, use_global_device_ids=true, to_apply=%region_2.3 | all-reduce | flops 640 | bytes 5120 | tf_op jit(solution)/shard_map/psum | solution.py:198
  71.3 0.2 convolution_bitcast_fusion
  71.5 0.6 copy.15
  (6 shorter events, 0.0 us)
Async XLA Ops:
  0.0 6.1 %copy-start = (s32[4,4]{1,0:T(4,128)S(1)}, s32[4,4]{1,0:T(4,128)}, u32[]{:S(2)}) copy-start(s32[4,4]{1,0:T(4,128)} %param.14) | copy-start | bytes 196
  0.9 9.4 %collective-permute-start = (bf16[2,64,512]{2,1,0:T(8,128)(2,1)S(1)}, bf16[2,64,512]{2,1,0:T(8,128)(2,1)S(1)}, u32[]{:S(2)}, u32[]{:S(2)}) collective-permute-start(bf16[2,64,512]{2,1,0:T(8,128)(2,1)S(1)} %pad_maximum_fusion.1), channel_id=1, source_target_pairs={{0,4},{4,8},{8,12},{12,0},{1,5},{5,9},{9,13},{13,1},{2,6},{6,10},{... | collective-permute-start | bytes 393224 | tf_op jit(solution)/shard_map/ppermute | solution.py:132
  4.0 7.8 %collective-permute-start.1 = (bf16[2,64,512]{2,1,0:T(8,128)(2,1)S(1)}, bf16[2,64,512]{2,1,0:T(8,128)(2,1)S(1)}, u32[]{:S(2)}, u32[]{:S(2)}) collective-permute-start(bf16[2,64,512]{2,1,0:T(8,128)(2,1)S(1)} %pad_maximum_fusion.1), channel_id=1, source_target_pairs={{4,0},{8,4},{12,8},{0,12},{5,1},{9,5},{13,9},{1,13},{6,2},{10,6},{... | collective-permute-start | bytes 393224 | tf_op jit(solution)/shard_map/ppermute | solution.py:133
  11.8 1.6 %copy-start.1 = (bf16[1,2,1024,512]{3,2,1,0:T(8,128)(2,1)S(1)}, bf16[1,2,1024,512]{3,2,1,0:T(8,128)(2,1)}, u32[]{:S(2)}) copy-start(bf16[1,2,1024,512]{3,2,1,0:T(8,128)(2,1)} %param.12) | copy-start | bytes 6291460
  13.4 1.0 %copy-start.4 = (f32[1024,1]{1,0:T(8,128)S(1)}, f32[1024,1]{1,0:T(8,128)}, u32[]{:S(2)}) copy-start(f32[1024,1]{1,0:T(8,128)} %constant.99.row_taper_ref) | copy-start | bytes 12292
  19.5 6.5 %copy-start.2 = (bf16[1024,512]{1,0:T(8,128)(2,1)S(1)}, bf16[1024,512]{1,0:T(8,128)(2,1)}, u32[]{:S(2)}) copy-start(bf16[1024,512]{1,0:T(8,128)(2,1)} %constant.92.clone.cos_ref) | copy-start | bytes 3145732
  19.5 6.5 %copy-start.3 = (bf16[1024,512]{1,0:T(8,128)(2,1)S(1)}, bf16[1024,512]{1,0:T(8,128)(2,1)}, u32[]{:S(2)}) copy-start(bf16[1024,512]{1,0:T(8,128)(2,1)} %constant.93.clone.sin_ref) | copy-start | bytes 3145732
  31.3 3.9 %copy-start.8 = (s32[4]{0:T(128)S(1)}, s32[4]{0:T(128)}, u32[]{:S(2)}) copy-start(s32[4]{0:T(128)} %param.16) | copy-start | bytes 52
  31.3 5.8 %copy-start.7 = (s32[129]{0:T(256)S(1)}, s32[129]{0:T(256)}, u32[]{:S(2)}) copy-start(s32[129]{0:T(256)} %param.18) | copy-start | bytes 1552
  31.3 6.4 %copy-start.9 = (u32[32]{0:T(128)S(1)}, u32[32]{0:T(128)}, u32[]{:S(2)}) copy-start(u32[32]{0:T(128)} %constant.102) | copy-start | bytes 388
  31.3 8.2 %copy-start.6 = (f32[1,128,128]{2,1,0:T(8,128)S(1)}, f32[1,128,128]{2,1,0:T(8,128)}, u32[]{:S(2)}) copy-start(f32[1,128,128]{2,1,0:T(8,128)} %param.17) | copy-start | bytes 196612
  31.3 29.3 %copy-start.5 = (bf16[256,128]{1,0:T(8,128)(2,1)S(1)}, bf16[256,128]{1,0:T(8,128)(2,1)}, u32[]{:S(2)}) copy-start(bf16[256,128]{1,0:T(8,128)(2,1)} %constant.94.clone.refs_4_) | copy-start | bytes 196612
  31.3 29.3 %all-to-all-start.1 = ((bf16[2,2,4,128,512]{4,3,2,1,0:T(8,128)(2,1)}), bf16[2,2,4,128,512]{4,3,2,1,0:T(8,128)(2,1)S(1)}, u32[]{:S(2)}, u32[]{:S(2)}) async-start(bf16[2,2,4,128,512]{4,3,2,1,0:T(8,128)(2,1)} %second_transform.1), calls=%async_computation.1 | async-start | bytes 4194304 | tf_op jit(solution)/shard_map/all_to_all | solution.py:180

commit v2 on v1

v2 whole, which is shorter than its diff:
```python
import math

import jax
import jax.numpy as jnp
import ml_dtypes
import numpy as np
from jax import lax
from jax.experimental import pallas as pl
from jax.experimental.pallas import tpu as pltpu
from jax.sharding import PartitionSpec as P

W = 32
APOD = 64
LANES = 128
MESH = pl.DeviceIdType.MESH


def taper_profile(length, ramp_width):
    position = np.arange(length)
    distance = np.minimum(position, length - 1 - position)
    ramped = 0.5 - 0.5 * np.cos(math.pi * (distance + 0.5) / ramp_width)
    return np.where(distance < ramp_width, ramped, 1.0).astype(np.float32)


def fourier_tables(length):
    half = length // 2
    phases = np.arange(half)[:, None] * np.arange(length)[None, :] % length
    angles = phases * (2.0 * math.pi / length)
    return (
        np.cos(angles).astype(np.float32).astype(ml_dtypes.bfloat16),
        np.sin(angles).astype(np.float32).astype(ml_dtypes.bfloat16),
    )


def edge_reach(edges, wave_rows):
    room = edges * edges - wave_rows * wave_rows
    reach = jnp.sqrt(jnp.maximum(room, 0).astype(jnp.float32)).astype(jnp.int32) - 1
    for _ in range(3):
        reach = reach + (reach * reach < room).astype(jnp.int32)
    return jnp.where(room > 0, reach, 0)


def kernel(
    sizes,
    src_ref, row_ref, count_ref, class_ref, edges_ref, ramp_ref, col_taper_ref, prefix_ref,
    maps_hbm, bank_hbm, table_hbm, turn_hbm,
    out_ref,
    maps, table, turn, strips, bank, tapered,
    cols_send, cols_own, cols_recv, modes_send, modes, discs, shares,
    load_sem, strip_send, strip_recv, bank_send, bank_recv, cols_ssem, cols_rsem,
    modes_ssem, modes_rsem, share_ssem, share_rsem,
):
    patches, zbins, freqs = sizes
    bins, length, columns = maps.shape
    half = length // 2
    rows_freq = half // freqs
    rows = rows_freq // zbins
    bins_total = bins * zbins
    pair_total = bins_total * (bins_total + 1) // 2
    pair_share = pair_total // zbins
    me = lax.axis_index("patch")
    z = lax.axis_index("zbin")
    f = lax.axis_index("freq")
    other = 1 - f
    right, left = lax.rem(me + 1, patches), lax.rem(me + patches - 1, patches)

    loads = [
        pltpu.make_async_copy(maps_hbm.at[0], maps, load_sem.at[0]),
        pltpu.make_async_copy(table_hbm, table, load_sem.at[1]),
        pltpu.make_async_copy(turn_hbm, turn, load_sem.at[2]),
        pltpu.make_async_copy(bank_hbm, bank.at[0], load_sem.at[3]),
    ]
    for load in loads:
        load.start()

    group = [(dz, df) for dz in range(zbins) for df in range(freqs) if (dz, df) != (0, 0)]
    barrier = pltpu.get_barrier_semaphore()
    for k in range(1, patches):
        pl.semaphore_signal(barrier, inc=1, device_id={"patch": lax.rem(me + k, patches)}, device_id_type=MESH)
    for dz, df in group:
        pl.semaphore_signal(
            barrier,
            inc=1,
            device_id={"zbin": lax.rem(z + dz, zbins), "freq": lax.rem(f + df, freqs)},
            device_id_type=MESH,
        )
    pl.semaphore_wait(barrier, patches - 1 + len(group))

    strip_copies = []
    for side, target in ((0, right), (1, left)):
        for s, at in ((0, 0), (1, length - W)):
            slot = side * 2 + s
            copy = pltpu.make_async_remote_copy(
                src_ref=maps_hbm.at[0, :, pl.ds(at, W), :],
                dst_ref=strips.at[:, slot],
                send_sem=strip_send.at[slot],
                recv_sem=strip_recv.at[slot],
                device_id={"patch": target},
                device_id_type=MESH,
            )
            copy.start()
            strip_copies.append(copy)

    discs[...] = jnp.zeros_like(discs)
    entries = []
    for k in range(src_ref.shape[1]):
        source = src_ref[me, k]
        side = jnp.where(lax.shift_right_logical(source, 1) == left, 0, 1)
        slot = (side * 2 + (source & 1)) * W
        live = k < count_ref[me]
        entries.append((jnp.where(live, slot, -length), row_ref[me, k]))
    place = lax.broadcasted_iota(jnp.int32, (1, 4 * W), 1)
    marks = []
    for slot, row in entries:
        at = place - slot
        marks.append(jnp.where((at >= 0) & (at < W), at + row, -1))

    loads[0].wait()
    for copy in strip_copies:
        copy.wait_recv()

    bank_copies = []
    for k in range(1, patches):
        copy = pltpu.make_async_remote_copy(
            src_ref=bank_hbm,
            dst_ref=bank.at[k],
            send_sem=bank_send.at[k],
            recv_sem=bank_recv.at[k],
            device_id={"patch": lax.rem(me + k, patches)},
            device_id_type=MESH,
        )
        copy.start()
        bank_copies.append(copy)

    col_taper = col_taper_ref[:, pl.ds(pl.multiple_of(f * columns, columns), columns)]
    bounds = [0, APOD] + list(range(4 * APOD, length - APOD, 4 * APOD)) + [length - APOD, length]
    for start, stop in zip(bounds[:-1], bounds[1:]):
        pixel = start + lax.broadcasted_iota(jnp.int32, (stop - start, 1), 0)
        pick = None
        for mark in marks:
            hit = (pixel == mark).astype(jnp.float32)
            pick = hit if pick is None else pick + hit
        pick = pick.astype(jnp.bfloat16)
        for b in range(bins):
            image = maps[b, pl.ds(start, stop - start), :].astype(jnp.float32) + jnp.dot(
                pick, strips[b].reshape(4 * W, columns), preferred_element_type=jnp.float32
            )
            if start == 0:
                image = image * ramp_ref[pl.ds(0, APOD), :]
            if stop == length:
                image = image * ramp_ref[pl.ds(APOD, APOD), :]
            tapered[b, pl.ds(start, stop - start), :] = (image * col_taper).astype(jnp.bfloat16)

    order = list(range(1, zbins)) + [0]
    loads[1].wait()

    def first_transform(half_index, d, target):
        base = half_index * rows_freq + lax.rem(z + d, zbins) * rows
        lhs = jnp.concatenate(
            [
                table[pl.ds(pl.multiple_of(base, rows), rows), :],
                table[pl.ds(pl.multiple_of(half + base, rows), rows), :],
            ],
            axis=0,
        )
        for b in range(bins):
            target[d, b] = jnp.dot(lhs, tapered[b], preferred_element_type=jnp.float32).astype(jnp.bfloat16)

    cols_copies = {}
    for d in order:
        first_transform(other, d, cols_send)
        copy = pltpu.make_async_remote_copy(
            src_ref=cols_send.at[d],
            dst_ref=cols_recv.at[d],
            send_sem=cols_ssem.at[d],
            recv_sem=cols_rsem.at[d],
            device_id={"freq": other},
            device_id_type=MESH,
        )
        copy.start()
        cols_copies[d] = copy

    def second_transform(d, b, store):
        own = pl.ds(pl.multiple_of(f * columns, columns), columns)
        far = pl.ds(pl.multiple_of(other * columns, columns), columns)
        both = [
            jnp.dot(cols_own[d, b], turn[t, own, :], preferred_element_type=jnp.float32)
            + jnp.dot(cols_recv[d, b], turn[t, far, :], preferred_element_type=jnp.float32)
            for t in range(2)
        ]
        real_cos, imag_cos = both[0][:rows], both[0][rows:]
        real_sin, imag_sin = both[1][:rows], both[1][rows:]
        store(0, (real_cos + imag_sin).astype(jnp.bfloat16))
        store(1, (real_cos - imag_sin).astype(jnp.bfloat16))
        store(2, (imag_cos - real_sin).astype(jnp.bfloat16))
        store(3, (imag_cos + real_sin).astype(jnp.bfloat16))

    modes_copies = {}
    for d in order:
        first_transform(f, d, cols_own)
        if d == order[0]:
            loads[2].wait()
        cols_copies[d].wait_recv()
        for b in range(bins):
            buffer = modes_send if d else modes

            def store(part, value, buffer=buffer, d=d, b=b):
                buffer[d, b, part] = value

            second_transform(d, b, store)
            if d:
                copy = pltpu.make_async_remote_copy(
                    src_ref=modes_send.at[d, b],
                    dst_ref=modes.at[d, b],
                    send_sem=modes_ssem.at[d, b],
                    recv_sem=modes_rsem.at[d, b],
                    device_id={"zbin": lax.rem(z + d, zbins)},
                    device_id_type=MESH,
                )
                copy.start()
                modes_copies[d, b] = copy

    wave_rows = f * rows_freq + z * rows + lax.broadcasted_iota(jnp.int32, (rows, LANES), 0)
    lane = lax.broadcasted_iota(jnp.int32, (rows, LANES), 1)
    lower_edges = edges_ref[pl.ds(0, 1), :]
    upper_edges = edges_ref[pl.ds(1, 1), :]
    low = lower_edges[:, :1]
    reach = edge_reach(upper_edges, wave_rows)

    def band_sums(pairs):
        for block in range(half // LANES):
            lanes = pl.ds(block * LANES, LANES)
            index = jnp.clip(reach - block * LANES, 1, LANES) - 1
            inside = reach > block * LANES
            wave_cols = lane + block * LANES
            scale = (wave_rows * wave_rows + wave_cols * wave_cols >= low * low).astype(jnp.float32)
            if block == 0:
                scale = scale * jnp.where(lane == 0, 0.5, 1.0)
            for (d1, b1), (d2, b2) in pairs:
                cross = None
                for c in range(4):
                    term = modes[d1, b1, c, :, lanes].astype(jnp.float32) * modes[
                        d2, b2, c, :, lanes
                    ].astype(jnp.float32)
                    cross = term if cross is None else cross + term
                cross = cross * scale
                upper = cross.astype(jnp.bfloat16)
                lower = (cross - upper.astype(jnp.float32)).astype(jnp.bfloat16)
                sums = jnp.dot(
                    jnp.concatenate([upper, lower], axis=1), prefix_ref[...], preferred_element_type=jnp.float32
                )
                taken = jnp.where(inside, jnp.take_along_axis(sums, index, axis=1), 0.0)
                g1 = lax.rem(z + zbins - d1, zbins) * bins + b1
                g2 = lax.rem(z + zbins - d2, zbins) * bins + b2
                first, second = jnp.minimum(g1, g2), jnp.maximum(g1, g2)
                number = first * bins_total - first * (first - 1) // 2 + second - first
                spot = number // pair_share
                line = pl.ds(number - spot * pair_share, 1)
                discs[spot, line, :] += jnp.sum(taken, axis=0, keepdims=True)

    bins_of = {d: [(d, b) for b in range(bins)] for d in range(zbins)}
    own = bins_of[0]
    band_sums([(own[i], own[j]) for i in range(bins) for j in range(i, bins)])

    counts = jnp.zeros((1, LANES), jnp.int32)
    for start in range(0, half, LANES):
        every = start + lax.broadcasted_iota(jnp.int32, (LANES, LANES), 0)
        inner = jnp.maximum(2 * edge_reach(lower_edges, every) - 1, 0)
        outer = jnp.maximum(2 * edge_reach(upper_edges, every) - 1, 0)
        counts = counts + jnp.sum(outer - inner, axis=0, keepdims=True)

    done = list(own)
    for d in range(1, zbins):
        for b in range(bins):
            modes_copies[d, b].wait_recv()
            done.append((d, b))
            band_sums([(old, (d, b)) for old in done])
    loads[3].wait()

    copies = []
    for n, (dz, df) in enumerate(group):
        target = lax.rem(z + dz, zbins)
        copy = pltpu.make_async_remote_copy(
            src_ref=discs.at[target],
            dst_ref=shares.at[n],
            send_sem=share_ssem.at[n],
            recv_sem=share_rsem.at[n],
            device_id={"zbin": target, "freq": lax.rem(f + df, freqs)},
            device_id_type=MESH,
        )
        copy.start()
        copies.append(copy)
    total = discs[z]
    for n, copy in enumerate(copies):
        copy.wait_recv()
        total = total + shares[n]
    for copy in bank_copies:
        copy.wait_recv()

    shifted = pltpu.roll(total, 1, 1)
    shifted = jnp.where(lax.broadcasted_iota(jnp.int32, total.shape, 1) == 0, 0.0, shifted)
    pseudo = (total - shifted) / (counts.astype(jnp.float32) * float(length * length))
    kind = class_ref[me]
    holder = kind // bank.shape[1]
    matrix = bank[lax.rem(me - holder + patches, patches), kind - holder * bank.shape[1]]
    result = lax.dot_general(
        pseudo,
        matrix,
        (((1,), (1,)), ((), ())),
        precision=lax.Precision.HIGHEST,
        preferred_element_type=jnp.float32,
    )
    out_ref[0] = result[:pair_share]

    for copy in strip_copies + bank_copies + list(cols_copies.values()) + list(modes_copies.values()) + copies:
        copy.wait_send()


def per_device(density_maps, margin_src, margin_row, margin_count, class_id, coupling_bank, band_edges):
    _, bins, length, columns = density_maps.shape
    half = length // 2
    freqs = lax.axis_size("freq")
    zbins = lax.axis_size("zbin")
    patches = lax.axis_size("patch")
    rows = half // freqs // zbins
    bins_total = bins * zbins
    pair_share = bins_total * (bins_total + 1) // 2 // zbins
    padded = -(-pair_share // 8) * 8
    group = zbins * freqs - 1

    profile = taper_profile(length, APOD)
    ramp = np.concatenate([profile[:APOD], profile[length - APOD :]])[:, None]
    cos_np, sin_np = fourier_tables(length)
    minus_sin = (-sin_np.astype(np.float32)).astype(ml_dtypes.bfloat16)
    table = np.concatenate([cos_np, minus_sin], axis=0)
    turn = np.stack([np.ascontiguousarray(cos_np.T), np.ascontiguousarray(sin_np.T)])
    ones = np.triu(np.ones((LANES, LANES)))
    prefix = np.concatenate([ones, ones], axis=0).astype(ml_dtypes.bfloat16)
    edges = jnp.stack([band_edges[:-1], band_edges[1:]])

    smem = pl.BlockSpec(memory_space=pltpu.SMEM)
    vmem = pl.BlockSpec(memory_space=pltpu.VMEM)
    anywhere = pl.BlockSpec(memory_space=pl.ANY)
    dma = pltpu.SemaphoreType.DMA
    bf16, f32 = jnp.bfloat16, jnp.float32
    sizes = (patches, zbins, freqs)
    return pl.pallas_call(
        lambda *refs: kernel(sizes, *refs),
        out_shape=jax.ShapeDtypeStruct((1, pair_share, LANES), f32),
        in_specs=[smem] * 4 + [vmem] * 4 + [anywhere] * 4,
        out_specs=vmem,
        scratch_shapes=[
            pltpu.VMEM((bins, length, columns), bf16),
            pltpu.VMEM((length, length), bf16),
            pltpu.VMEM((2, length, half), bf16),
            pltpu.VMEM((bins, 4, W, columns), bf16),
            pltpu.VMEM((patches,) + coupling_bank.shape, f32),
            pltpu.VMEM((bins, length, columns), bf16),
            pltpu.VMEM((zbins, bins, 2 * rows, columns), bf16),
            pltpu.VMEM((zbins, bins, 2 * rows, columns), bf16),
            pltpu.VMEM((zbins, bins, 2 * rows, columns), bf16),
            pltpu.VMEM((zbins, bins, 4, rows, half), bf16),
            pltpu.VMEM((zbins, bins, 4, rows, half), bf16),
            pltpu.VMEM((zbins, padded, LANES), f32),
            pltpu.VMEM((group, padded, LANES), f32),
            dma((4,)), dma((4,)), dma((4,)), dma((patches,)), dma((patches,)), dma((zbins,)), dma((zbins,)),
            dma((zbins, bins)), dma((zbins, bins)), dma((group,)), dma((group,)),
        ],
        compiler_params=pltpu.CompilerParams(
            collective_id=0, has_side_effects=True, vmem_limit_bytes=56 * 1024 * 1024
        ),
        name="spectra",
    )(
        margin_src, margin_row, margin_count, class_id, edges, jnp.asarray(ramp),
        jnp.asarray(profile)[None, :], jnp.asarray(prefix),
        density_maps, coupling_bank, jnp.asarray(table), jnp.asarray(turn),
    )


def solution(mesh):
    in_specs = (
        P(("groups", "patch"), "zbin", None, "freq"),
        P("groups", None),
        P("groups", None),
        P("groups"),
        P("groups"),
        P("patch", None, None),
        P(),
    )
    out_specs = P(("groups", "patch"), "zbin", None)
    return jax.shard_map(
        per_device, mesh=mesh, in_specs=in_specs, out_specs=out_specs, check_vma=False
    )
```

time: 72.8 us -> 48.9 us (0.67)
  Pallas kernels: 13.5 us -> 46 us
  blocking collectives: 27.7 us -> 0 us
  starting transfers between devices: 9.07 us -> 0 us
  waiting for transfers between devices: 8.36 us -> 0 us
  local copies, waits for them, and re-layouts: 7.97 us -> 2.08 us
  between operations: 2.65 us -> 0.01 us
  other arithmetic: 2.57 us -> 0.57 us
    pallas_call x3 -> x1, Pallas kernels: 13.5 us -> 46 us  [per_device(): pl.pallas_call(lambda *refs: kernel(sizes, *refs), out_shape=jax.ShapeDty...]
    all_gather x1 -> x0, blocking collectives: 13.8 us -> none  [per_device(): bank = lax.all_gather(coupling_bank, 'patch', axis=0, tiled=True)]
    all_to_all x1 -> x0, waiting for transfers between devices: 6.71 us -> none  [per_device(): lax.all_to_all(modes, 'zbin', split_axis=0, concat_axis=0, tiled=True)]
    all_to_all x1 -> x0, blocking collectives: 6.45 us -> none  [per_device(): cols = lax.all_to_all(cols, 'freq', split_axis=0, concat_axis=0, tiled=True)]
    ppermute x2 -> x0, starting transfers between devices: 5.17 us -> none  [the longest x1 3.08 us: per_device(): lax.ppermute(strips, 'patch', [(i, (i + 1) % patch_count) for i in range(...]
    unnamed x1 -> x0, blocking collectives: 5.01 us -> none
    all_to_all x1 -> x0, starting transfers between devices: 3.91 us -> none  [per_device(): lax.all_to_all(modes, 'zbin', split_axis=0, concat_axis=0, tiled=True)]
    unnamed x22 -> x0, local copies, waits for them, and re-layouts: 3.25 us -> none
  transfers between devices with their start and end apart: 3 -> 0, of which waited for: 3 -> 0; matrix products, arithmetic and copies ran while one was open for 9% -> 0% of each run, Pallas kernels for 0% -> 0%
where the time goes in v2:
time: 48.9 us; the launch traced here: 48.7 us
  Pallas kernels  46 us (94%)
  local copies, waits for them, and re-layouts  2.08 us (4%)
  other arithmetic  0.57 us (1%)
    pallas_call x1, Pallas kernels, per_device(): pl.pallas_call(lambda *refs: kernel(sizes, *refs), out_shape=jax.ShapeDty...  46 us
    pallas_call x1, local copies, waits for them, and re-layouts, per_device(): pl.pallas_call(lambda *refs: kernel(sizes, *refs), out_shape=jax.ShapeDty...  1.25 us

profile of v2, /device:TPU:0, one launch (start us, length us, event | category | flops | bytes accessed | tf_op | source)
XLA Modules:
  0.0 48.7 jit_solution(16565167599250969662)
XLA Ops:
  0.0 0.8 %slice_bitcast_fusion.1 = (s32[1,128]{1,0:T(1,128)S(1)}, s32[1,128]{1,0:T(1,128)S(1)}) fusion(s32[129]{0:T(256)} %param.18), kind=kLoop, calls=%fused_computation.2 | loop fusion | bytes 2048 | tf_op jit(solution)/shard_map/stack | solution.py:339
  0.8 0.6 %pad_add_fusion.refs_4_ = s32[2,128]{1,0:T(2,128)} fusion(s32[1,128]{1,0:T(1,128)S(1)} %get-tuple-element.6, s32[1,128]{1,0:T(1,128)S(1)} %get-tuple-element.5), kind=kLoop, calls=%fused_computation | loop fusion | flops 256 | bytes 2048 | tf_op jit(solution)/shard_map/stack | solution.py:339
  1.4 46.0 %spectra.1 = f32[1,5,128]{2,1,0:T(8,128)} custom-call(s32[4,4]{1,0:T(4,128)} %refs_0_.1, s32[4,4]{1,0:T(4,128)} %refs_1_.1, s32[4]{0:T(128)} %refs_2_.1, s32[4]{0:T(128)} %refs_3_.1, s32[2,128]{1,0:T(2,128)} %pad_add_fusion.refs_4_, f32[128,1]{1,0:T(8,128)} %constant.10.clone.refs_5_, f32[1,1024]{1,0:T(1,128)} %constant.17.refs_6_, ...), custom_call_target="tpu_custom_call" | custom-call | tf_op jit(solution)/shard_map/spectra/pallas_call | solution.py:347
  47.4 1.3 %copy.13 = f32[1,5,128]{2,0,1:T(1,128)} copy(f32[1,5,128]{2,1,0:T(8,128)} %spectra.1) | data formatting | bytes 5120 | tf_op jit(solution)/shard_map/spectra/pallas_call | solution.py:347

commit v3 on v2

--- a/solution.py
+++ b/solution.py
@@ -10,6 +10,7 @@
 from jax.sharding import PartitionSpec as P
 
 W = 32
+BLOCK = 16
 APOD = 64
 LANES = 128
 MESH = pl.DeviceIdType.MESH
@@ -119,19 +120,6 @@
     for copy in strip_copies:
         copy.wait_recv()
 
-    bank_copies = []
-    for k in range(1, patches):
-        copy = pltpu.make_async_remote_copy(
-            src_ref=bank_hbm,
-            dst_ref=bank.at[k],
-            send_sem=bank_send.at[k],
-            recv_sem=bank_recv.at[k],
-            device_id={"patch": lax.rem(me + k, patches)},
-            device_id_type=MESH,
-        )
-        copy.start()
-        bank_copies.append(copy)
-
     col_taper = col_taper_ref[:, pl.ds(pl.multiple_of(f * columns, columns), columns)]
     bounds = [0, APOD] + list(range(4 * APOD, length - APOD, 4 * APOD)) + [length - APOD, length]
     for start, stop in zip(bounds[:-1], bounds[1:]):
@@ -152,6 +140,12 @@
             tapered[b, pl.ds(start, stop - start), :] = (image * col_taper).astype(jnp.bfloat16)
 
     order = list(range(1, zbins)) + [0]
+    blocks = half // LANES
+    spread = freqs * zbins * BLOCK
+    heights = [
+        BLOCK * sum((at * LANES) ** 2 + (t * spread) ** 2 < (half - 1) ** 2 for t in range(rows // BLOCK))
+        for at in range(blocks)
+    ]
     loads[1].wait()
 
     def first_transform(half_index, d, target):
@@ -164,9 +158,27 @@
             axis=0,
         )
         for b in range(bins):
-            target[d, b] = jnp.dot(lhs, tapered[b], preferred_element_type=jnp.float32).astype(jnp.bfloat16)
-
-    cols_copies = {}
+            target[d, pl.ds(b * 2 * rows, 2 * rows), :] = jnp.dot(
+                lhs, tapered[b], preferred_element_type=jnp.float32
+            ).astype(jnp.bfloat16)
+
+    def second_transform(d, at, target):
+        own = pl.ds(pl.multiple_of(f * columns, columns), columns)
+        far = pl.ds(pl.multiple_of(other * columns, columns), columns)
+        both = jnp.dot(cols_own[d], turn[at, own, :], preferred_element_type=jnp.float32) + jnp.dot(
+            cols_recv[d], turn[at, far, :], preferred_element_type=jnp.float32
+        )
+        for b in range(bins):
+            real = both[b * 2 * rows : (2 * b + 1) * rows]
+            imag = both[(2 * b + 1) * rows : (2 * b + 2) * rows]
+            real_cos, real_sin = real[:, :LANES], real[:, LANES:]
+            imag_cos, imag_sin = imag[:, :LANES], imag[:, LANES:]
+            target[d, at, b, 0] = (real_cos + imag_sin).astype(jnp.bfloat16)
+            target[d, at, b, 1] = (real_cos - imag_sin).astype(jnp.bfloat16)
+            target[d, at, b, 2] = (imag_cos - real_sin).astype(jnp.bfloat16)
+            target[d, at, b, 3] = (imag_cos + real_sin).astype(jnp.bfloat16)
+
+    cols_copies, modes_copies = {}, {}
     for d in order:
         first_transform(other, d, cols_send)
         copy = pltpu.make_async_remote_copy(
@@ -179,88 +191,81 @@
         )
         copy.start()
         cols_copies[d] = copy
-
-    def second_transform(d, b, store):
-        own = pl.ds(pl.multiple_of(f * columns, columns), columns)
-        far = pl.ds(pl.multiple_of(other * columns, columns), columns)
-        both = [
-            jnp.dot(cols_own[d, b], turn[t, own, :], preferred_element_type=jnp.float32)
-            + jnp.dot(cols_recv[d, b], turn[t, far, :], preferred_element_type=jnp.float32)
-            for t in range(2)
-        ]
-        real_cos, imag_cos = both[0][:rows], both[0][rows:]
-        real_sin, imag_sin = both[1][:rows], both[1][rows:]
-        store(0, (real_cos + imag_sin).astype(jnp.bfloat16))
-        store(1, (real_cos - imag_sin).astype(jnp.bfloat16))
-        store(2, (imag_cos - real_sin).astype(jnp.bfloat16))
-        store(3, (imag_cos + real_sin).astype(jnp.bfloat16))
-
-    modes_copies = {}
-    for d in order:
         first_transform(f, d, cols_own)
         if d == order[0]:
             loads[2].wait()
-        cols_copies[d].wait_recv()
-        for b in range(bins):
-            buffer = modes_send if d else modes
-
-            def store(part, value, buffer=buffer, d=d, b=b):
-                buffer[d, b, part] = value
-
-            second_transform(d, b, store)
+        copy.wait_recv()
+        for at in range(blocks):
+            second_transform(d, at, modes_send if d else modes)
             if d:
+                part = pl.ds(0, heights[at])
                 copy = pltpu.make_async_remote_copy(
-                    src_ref=modes_send.at[d, b],
-                    dst_ref=modes.at[d, b],
-                    send_sem=modes_ssem.at[d, b],
-                    recv_sem=modes_rsem.at[d, b],
+                    src_ref=modes_send.at[d, at, :, :, part, :],
+                    dst_ref=modes.at[d, at, :, :, part, :],
+                    send_sem=modes_ssem.at[d, at],
+                    recv_sem=modes_rsem.at[d, at],
                     device_id={"zbin": lax.rem(z + d, zbins)},
                     device_id_type=MESH,
                 )
                 copy.start()
-                modes_copies[d, b] = copy
-
-    wave_rows = f * rows_freq + z * rows + lax.broadcasted_iota(jnp.int32, (rows, LANES), 0)
+                modes_copies[d, at] = copy
+
+    bank_copies = []
+    for k in range(1, patches):
+        copy = pltpu.make_async_remote_copy(
+            src_ref=bank_hbm,
+            dst_ref=bank.at[k],
+            send_sem=bank_send.at[k],
+            recv_sem=bank_recv.at[k],
+            device_id={"patch": lax.rem(me + k, patches)},
+            device_id_type=MESH,
+        )
+        copy.start()
+        bank_copies.append(copy)
+
+    local_row = lax.broadcasted_iota(jnp.int32, (rows, LANES), 0)
+    wave_rows = (local_row // BLOCK * (freqs * zbins) + f * zbins + z) * BLOCK + local_row % BLOCK
     lane = lax.broadcasted_iota(jnp.int32, (rows, LANES), 1)
-    lower_edges = edges_ref[pl.ds(0, 1), :]
-    upper_edges = edges_ref[pl.ds(1, 1), :]
+    lower_edges = edges_ref[pl.ds(0, LANES)].reshape(1, LANES)
+    upper_edges = edges_ref[pl.ds(1, LANES)].reshape(1, LANES)
     low = lower_edges[:, :1]
     reach = edge_reach(upper_edges, wave_rows)
 
-    def band_sums(pairs):
-        for block in range(half // LANES):
-            lanes = pl.ds(block * LANES, LANES)
-            index = jnp.clip(reach - block * LANES, 1, LANES) - 1
-            inside = reach > block * LANES
-            wave_cols = lane + block * LANES
-            scale = (wave_rows * wave_rows + wave_cols * wave_cols >= low * low).astype(jnp.float32)
-            if block == 0:
-                scale = scale * jnp.where(lane == 0, 0.5, 1.0)
-            for (d1, b1), (d2, b2) in pairs:
-                cross = None
-                for c in range(4):
-                    term = modes[d1, b1, c, :, lanes].astype(jnp.float32) * modes[
-                        d2, b2, c, :, lanes
-                    ].astype(jnp.float32)
-                    cross = term if cross is None else cross + term
-                cross = cross * scale
-                upper = cross.astype(jnp.bfloat16)
-                lower = (cross - upper.astype(jnp.float32)).astype(jnp.bfloat16)
-                sums = jnp.dot(
-                    jnp.concatenate([upper, lower], axis=1), prefix_ref[...], preferred_element_type=jnp.float32
+    def band_sums(at, pairs):
+        height = heights[at]
+        index = (jnp.clip(reach - at * LANES, 1, LANES) - 1)[:height]
+        inside = (reach > at * LANES)[:height]
+        wave_cols = lane + at * LANES
+        scale = (wave_rows * wave_rows + wave_cols * wave_cols >= low * low).astype(jnp.float32)
+        if at == 0:
+            scale = scale * jnp.where(lane == 0, 0.5, 1.0)
+        scale = scale[:height]
+        part = pl.ds(0, height)
+        for (d1, b1), (d2, b2) in pairs:
+            cross = None
+            for c in range(4):
+                term = modes[d1, at, b1, c, part, :].astype(jnp.float32) * modes[d2, at, b2, c, part, :].astype(
+                    jnp.float32
                 )
-                taken = jnp.where(inside, jnp.take_along_axis(sums, index, axis=1), 0.0)
-                g1 = lax.rem(z + zbins - d1, zbins) * bins + b1
-                g2 = lax.rem(z + zbins - d2, zbins) * bins + b2
-                first, second = jnp.minimum(g1, g2), jnp.maximum(g1, g2)
-                number = first * bins_total - first * (first - 1) // 2 + second - first
-                spot = number // pair_share
-                line = pl.ds(number - spot * pair_share, 1)
-                discs[spot, line, :] += jnp.sum(taken, axis=0, keepdims=True)
-
-    bins_of = {d: [(d, b) for b in range(bins)] for d in range(zbins)}
-    own = bins_of[0]
-    band_sums([(own[i], own[j]) for i in range(bins) for j in range(i, bins)])
+                cross = term if cross is None else cross + term
+            cross = cross * scale
+            upper = cross.astype(jnp.bfloat16)
+            lower = (cross - upper.astype(jnp.float32)).astype(jnp.bfloat16)
+            sums = jnp.dot(
+                jnp.concatenate([upper, lower], axis=1), prefix_ref[...], preferred_element_type=jnp.float32
+            )
+            taken = jnp.where(inside, jnp.take_along_axis(sums, index, axis=1), 0.0)
+            g1 = lax.rem(z + zbins - d1, zbins) * bins + b1
+            g2 = lax.rem(z + zbins - d2, zbins) * bins + b2
+            first, second = jnp.minimum(g1, g2), jnp.maximum(g1, g2)
+            number = first * bins_total - first * (first - 1) // 2 + second - first
+            spot = number // pair_share
+            line = pl.ds(number - spot * pair_share, 1)
+            discs[spot, line, :] += jnp.sum(taken, axis=0, keepdims=True)
+
+    done = [(0, b) for b in range(bins)]
+    for at in range(blocks):
+        band_sums(at, [(done[i], done[j]) for i in range(bins) for j in range(i, bins)])
 
     counts = jnp.zeros((1, LANES), jnp.int32)
     for start in range(0, half, LANES):
@@ -269,12 +274,14 @@
         outer = jnp.maximum(2 * edge_reach(upper_edges, every) - 1, 0)
         counts = counts + jnp.sum(outer - inner, axis=0, keepdims=True)
 
-    done = list(own)
     for d in range(1, zbins):
-        for b in range(bins):
-            modes_copies[d, b].wait_recv()
-            done.append((d, b))
-            band_sums([(old, (d, b)) for old in done])
+        new = [(d, b) for b in range(bins)]
+        pairs = [(a, c) for a in done for c in new]
+        pairs += [(new[i], new[j]) for i in range(bins) for j in range(i, bins)]
+        for at in range(blocks):
+            modes_copies[d, at].wait_recv()
+            band_sums(at, pairs)
+        done += new
     loads[3].wait()
 
     copies = []
@@ -310,7 +317,8 @@
         precision=lax.Precision.HIGHEST,
         preferred_element_type=jnp.float32,
     )
-    out_ref[0] = result[:pair_share]
+    for q in range(pair_share):
+        out_ref[q] = result[q : q + 1]
 
     for copy in strip_copies + bank_copies + list(cols_copies.values()) + list(modes_copies.values()) + copies:
         copy.wait_send()
@@ -327,16 +335,23 @@
     pair_share = bins_total * (bins_total + 1) // 2 // zbins
     padded = -(-pair_share // 8) * 8
     group = zbins * freqs - 1
+    blocks = half // LANES
 
     profile = taper_profile(length, APOD)
     ramp = np.concatenate([profile[:APOD], profile[length - APOD :]])[:, None]
     cos_np, sin_np = fourier_tables(length)
     minus_sin = (-sin_np.astype(np.float32)).astype(ml_dtypes.bfloat16)
-    table = np.concatenate([cos_np, minus_sin], axis=0)
-    turn = np.stack([np.ascontiguousarray(cos_np.T), np.ascontiguousarray(sin_np.T)])
+    spot = np.arange(half)
+    dealt = (spot % rows // BLOCK * (freqs * zbins) + spot // rows) * BLOCK + spot % BLOCK
+    table = np.concatenate([cos_np[dealt], minus_sin[dealt]], axis=0)
+    turn = np.stack(
+        [
+            np.concatenate([cos_np.T[:, at : at + LANES], sin_np.T[:, at : at + LANES]], axis=1)
+            for at in range(0, half, LANES)
+        ]
+    )
     ones = np.triu(np.ones((LANES, LANES)))
     prefix = np.concatenate([ones, ones], axis=0).astype(ml_dtypes.bfloat16)
-    edges = jnp.stack([band_edges[:-1], band_edges[1:]])
 
     smem = pl.BlockSpec(memory_space=pltpu.SMEM)
     vmem = pl.BlockSpec(memory_space=pltpu.VMEM)
@@ -344,37 +359,38 @@
     dma = pltpu.SemaphoreType.DMA
     bf16, f32 = jnp.bfloat16, jnp.float32
     sizes = (patches, zbins, freqs)
-    return pl.pallas_call(
+    spectra = pl.pallas_call(
         lambda *refs: kernel(sizes, *refs),
-        out_shape=jax.ShapeDtypeStruct((1, pair_share, LANES), f32),
+        out_shape=jax.ShapeDtypeStruct((pair_share, 1, LANES), f32),
         in_specs=[smem] * 4 + [vmem] * 4 + [anywhere] * 4,
         out_specs=vmem,
         scratch_shapes=[
             pltpu.VMEM((bins, length, columns), bf16),
             pltpu.VMEM((length, length), bf16),
-            pltpu.VMEM((2, length, half), bf16),
+            pltpu.VMEM((blocks, length, 2 * LANES), bf16),
             pltpu.VMEM((bins, 4, W, columns), bf16),
             pltpu.VMEM((patches,) + coupling_bank.shape, f32),
             pltpu.VMEM((bins, length, columns), bf16),
-            pltpu.VMEM((zbins, bins, 2 * rows, columns), bf16),
-            pltpu.VMEM((zbins, bins, 2 * rows, columns), bf16),
-            pltpu.VMEM((zbins, bins, 2 * rows, columns), bf16),
-            pltpu.VMEM((zbins, bins, 4, rows, half), bf16),
-            pltpu.VMEM((zbins, bins, 4, rows, half), bf16),
+            pltpu.VMEM((zbins, bins * 2 * rows, columns), bf16),
+            pltpu.VMEM((zbins, bins * 2 * rows, columns), bf16),
+            pltpu.VMEM((zbins, bins * 2 * rows, columns), bf16),
+            pltpu.VMEM((zbins, blocks, bins, 4, rows, LANES), bf16),
+            pltpu.VMEM((zbins, blocks, bins, 4, rows, LANES), bf16),
             pltpu.VMEM((zbins, padded, LANES), f32),
             pltpu.VMEM((group, padded, LANES), f32),
             dma((4,)), dma((4,)), dma((4,)), dma((patches,)), dma((patches,)), dma((zbins,)), dma((zbins,)),
-            dma((zbins, bins)), dma((zbins, bins)), dma((group,)), dma((group,)),
+            dma((zbins, blocks)), dma((zbins, blocks)), dma((group,)), dma((group,)),
         ],
         compiler_params=pltpu.CompilerParams(
             collective_id=0, has_side_effects=True, vmem_limit_bytes=56 * 1024 * 1024
         ),
         name="spectra",
     )(
-        margin_src, margin_row, margin_count, class_id, edges, jnp.asarray(ramp),
+        margin_src, margin_row, margin_count, class_id, band_edges, jnp.asarray(ramp),
         jnp.asarray(profile)[None, :], jnp.asarray(prefix),
         density_maps, coupling_bank, jnp.asarray(table), jnp.asarray(turn),
     )
+    return jnp.transpose(spectra, (1, 0, 2))
 
 
 def solution(mesh):

time: 48.9 us -> 44.1 us (0.902)
  Pallas kernels: 46 us -> 42.7 us
  local copies, waits for them, and re-layouts: 2.08 us -> 1.26 us
  other arithmetic: 0.57 us -> 0 us
    pallas_call x1, Pallas kernels: 46 us -> 42.7 us  [per_device(): pl.pallas_call(lambda *refs: kernel(sizes, *refs), out_shape=jax.ShapeDty...]
    unnamed x0 -> x1, local copies, waits for them, and re-layouts: none -> 1.26 us
    pallas_call x1 -> x0, local copies, waits for them, and re-layouts: 1.25 us -> none  [per_device(): pl.pallas_call(lambda *refs: kernel(sizes, *refs), out_shape=jax.ShapeDty...]
    another operation x1 -> x0, local copies, waits for them, and re-layouts: 0.82 us -> none  [per_device(): edges = jnp.stack([band_edges[:-1], band_edges[1:]])]
    another operation x1 -> x0, other arithmetic: 0.57 us -> none  [per_device(): edges = jnp.stack([band_edges[:-1], band_edges[1:]])]
where the time goes in v3:
time: 44.1 us; the launch traced here: 44 us
  Pallas kernels  42.7 us (97%)
  local copies, waits for them, and re-layouts  1.26 us (3%)
    pallas_call x1, Pallas kernels, per_device(): pl.pallas_call(lambda *refs: kernel(sizes, *refs), out_shape=jax.ShapeDty...  42.7 us
    unnamed x1, local copies, waits for them, and re-layouts  1.26 us

profile of v3, /device:TPU:0, one launch (start us, length us, event | category | flops | bytes accessed | tf_op | source)
XLA Modules:
  0.0 44.0 jit_solution(9579179565660584519)
XLA Ops:
  0.0 42.7 %spectra.1 = f32[5,1,128]{2,1,0:T(1,128)} custom-call(s32[4,4]{1,0:T(4,128)} %refs_0_.1, s32[4,4]{1,0:T(4,128)} %refs_1_.1, s32[4]{0:T(128)} %refs_2_.1, s32[4]{0:T(128)} %refs_3_.1, s32[129]{0:T(256)} %refs_4_.1, f32[128,1]{1,0:T(8,128)} %constant.10.clone.refs_5_, f32[1,1024]{1,0:T(1,128)} %constant.17.refs_6_, bf16[256,128]{1,0:T(8,128)(2,1)} %constant.12.clone.refs_7_, ...), custom_call_target="tpu_custom_call" | custom-call | tf_op jit(solution)/shard_map/spectra/pallas_call | solution.py:362
  42.7 1.3 %copy.14 = f32[1,5,128]{2,0,1:T(1,128)} copy(f32[1,5,128]{2,0,1:T(1,128)} %bitcast.1) | data formatting | bytes 5120

commit v4 on v3

--- a/solution.py
+++ b/solution.py
@@ -47,7 +47,7 @@
     maps_hbm, bank_hbm, table_hbm, turn_hbm,
     out_ref,
     maps, table, turn, strips, bank, tapered,
-    cols_send, cols_own, cols_recv, modes_send, modes, discs, shares,
+    waiting, strip_table, strip_rows, cols_send, cols_own, cols_recv, modes_send, modes, discs, shares,
     load_sem, strip_send, strip_recv, bank_send, bank_recv, cols_ssem, cols_rsem,
     modes_ssem, modes_rsem, share_ssem, share_rsem,
 ):
@@ -107,32 +107,21 @@
     for k in range(src_ref.shape[1]):
         source = src_ref[me, k]
         side = jnp.where(lax.shift_right_logical(source, 1) == left, 0, 1)
-        slot = (side * 2 + (source & 1)) * W
-        live = k < count_ref[me]
-        entries.append((jnp.where(live, slot, -length), row_ref[me, k]))
-    place = lax.broadcasted_iota(jnp.int32, (1, 4 * W), 1)
-    marks = []
-    for slot, row in entries:
-        at = place - slot
-        marks.append(jnp.where((at >= 0) & (at < W), at + row, -1))
-
+        entries.append((side * 2 + (source & 1), k < count_ref[me], row_ref[me, k]))
+    def entry_rows(shape, axis):
+        place = lax.broadcasted_iota(jnp.int32, shape, axis)
+        rows_at = jnp.full(shape, -1, jnp.int32)
+        for k, (_, live, row) in enumerate(entries):
+            rows_at = jnp.where((place // W == k) & live, row + place % W, rows_at)
+        return rows_at
+
+    slots = len(entries) * W
     loads[0].wait()
-    for copy in strip_copies:
-        copy.wait_recv()
-
     col_taper = col_taper_ref[:, pl.ds(pl.multiple_of(f * columns, columns), columns)]
     bounds = [0, APOD] + list(range(4 * APOD, length - APOD, 4 * APOD)) + [length - APOD, length]
     for start, stop in zip(bounds[:-1], bounds[1:]):
-        pixel = start + lax.broadcasted_iota(jnp.int32, (stop - start, 1), 0)
-        pick = None
-        for mark in marks:
-            hit = (pixel == mark).astype(jnp.float32)
-            pick = hit if pick is None else pick + hit
-        pick = pick.astype(jnp.bfloat16)
-        for b in range(bins):
-            image = maps[b, pl.ds(start, stop - start), :].astype(jnp.float32) + jnp.dot(
-                pick, strips[b].reshape(4 * W, columns), preferred_element_type=jnp.float32
-            )
+        for b in range(bins):
+            image = maps[b, pl.ds(start, stop - start), :].astype(jnp.float32)
             if start == 0:
                 image = image * ramp_ref[pl.ds(0, APOD), :]
             if stop == length:
@@ -148,67 +137,93 @@
     ]
     loads[1].wait()
 
-    def first_transform(half_index, d, target):
+    def rows_of(ref, half_index, d):
         base = half_index * rows_freq + lax.rem(z + d, zbins) * rows
-        lhs = jnp.concatenate(
+        return jnp.concatenate(
             [
-                table[pl.ds(pl.multiple_of(base, rows), rows), :],
-                table[pl.ds(pl.multiple_of(half + base, rows), rows), :],
+                ref[pl.ds(pl.multiple_of(base, rows), rows), :],
+                ref[pl.ds(pl.multiple_of(half + base, rows), rows), :],
             ],
             axis=0,
         )
-        for b in range(bins):
-            target[d, pl.ds(b * 2 * rows, 2 * rows), :] = jnp.dot(
-                lhs, tapered[b], preferred_element_type=jnp.float32
-            ).astype(jnp.bfloat16)
-
-    def second_transform(d, at, target):
+
+    def base_product(half_index, d, b):
+        return jnp.dot(rows_of(table, half_index, d), tapered[b], preferred_element_type=jnp.float32)
+
+    def strip_product(half_index, d, b):
+        return jnp.dot(rows_of(strip_table, half_index, d), strip_rows[b], preferred_element_type=jnp.float32)
+
+    early = order[0]
+    for part, half_index in enumerate((other, f)):
+        for b in range(bins):
+            waiting[part, b] = base_product(half_index, early, b)
+    pixel = lax.broadcasted_iota(jnp.int32, (length, slots), 0)
+    pick = (pixel == entry_rows((1, slots), 1)).astype(jnp.float32).astype(jnp.bfloat16)
+    strip_table[...] = jnp.dot(table[...], pick, preferred_element_type=jnp.float32).astype(jnp.bfloat16)
+    across = lax.broadcasted_iota(jnp.int32, (slots, length), 1)
+    found = across == entry_rows((slots, 1), 0)
+    strip_taper = jnp.sum(jnp.where(found, col_taper_ref[...], 0.0), axis=1, keepdims=True)
+
+    for copy in strip_copies:
+        copy.wait_recv()
+    for b in range(bins):
+        for k, (slot, _, _) in enumerate(entries):
+            strip = strips[b, slot].astype(jnp.float32) * strip_taper[k * W : (k + 1) * W]
+            strip_rows[b, pl.ds(k * W, W), :] = (strip * col_taper).astype(jnp.bfloat16)
+
+    def second_transform(d, b, at, target):
         own = pl.ds(pl.multiple_of(f * columns, columns), columns)
         far = pl.ds(pl.multiple_of(other * columns, columns), columns)
-        both = jnp.dot(cols_own[d], turn[at, own, :], preferred_element_type=jnp.float32) + jnp.dot(
-            cols_recv[d], turn[at, far, :], preferred_element_type=jnp.float32
-        )
-        for b in range(bins):
-            real = both[b * 2 * rows : (2 * b + 1) * rows]
-            imag = both[(2 * b + 1) * rows : (2 * b + 2) * rows]
-            real_cos, real_sin = real[:, :LANES], real[:, LANES:]
-            imag_cos, imag_sin = imag[:, :LANES], imag[:, LANES:]
-            target[d, at, b, 0] = (real_cos + imag_sin).astype(jnp.bfloat16)
-            target[d, at, b, 1] = (real_cos - imag_sin).astype(jnp.bfloat16)
-            target[d, at, b, 2] = (imag_cos - real_sin).astype(jnp.bfloat16)
-            target[d, at, b, 3] = (imag_cos + real_sin).astype(jnp.bfloat16)
+        both = jnp.dot(cols_own[d, b], turn[at, own, :], preferred_element_type=jnp.float32) + jnp.dot(
+            cols_recv[d, b], turn[at, far, :], preferred_element_type=jnp.float32
+        )
+        real_cos, real_sin = both[:rows, :LANES], both[:rows, LANES:]
+        imag_cos, imag_sin = both[rows:, :LANES], both[rows:, LANES:]
+        target[d, at, b, 0] = (real_cos + imag_sin).astype(jnp.bfloat16)
+        target[d, at, b, 1] = (real_cos - imag_sin).astype(jnp.bfloat16)
+        target[d, at, b, 2] = (imag_cos - real_sin).astype(jnp.bfloat16)
+        target[d, at, b, 3] = (imag_cos + real_sin).astype(jnp.bfloat16)
 
     cols_copies, modes_copies = {}, {}
-    for d in order:
-        first_transform(other, d, cols_send)
+
+    def send_cols(d, b):
         copy = pltpu.make_async_remote_copy(
-            src_ref=cols_send.at[d],
-            dst_ref=cols_recv.at[d],
-            send_sem=cols_ssem.at[d],
-            recv_sem=cols_rsem.at[d],
+            src_ref=cols_send.at[d, b],
+            dst_ref=cols_recv.at[d, b],
+            send_sem=cols_ssem.at[d, b],
+            recv_sem=cols_rsem.at[d, b],
             device_id={"freq": other},
             device_id_type=MESH,
         )
         copy.start()
-        cols_copies[d] = copy
-        first_transform(f, d, cols_own)
-        if d == order[0]:
+        cols_copies[d, b] = copy
+
+    for d in order:
+        for b in range(bins):
+            base = waiting[0, b] if d == early else base_product(other, d, b)
+            cols_send[d, b] = (base + strip_product(other, d, b)).astype(jnp.bfloat16)
+            send_cols(d, b)
+        for b in range(bins):
+            base = waiting[1, b] if d == early else base_product(f, d, b)
+            cols_own[d, b] = (base + strip_product(f, d, b)).astype(jnp.bfloat16)
+        if d == early:
             loads[2].wait()
-        copy.wait_recv()
-        for at in range(blocks):
-            second_transform(d, at, modes_send if d else modes)
-            if d:
-                part = pl.ds(0, heights[at])
-                copy = pltpu.make_async_remote_copy(
-                    src_ref=modes_send.at[d, at, :, :, part, :],
-                    dst_ref=modes.at[d, at, :, :, part, :],
-                    send_sem=modes_ssem.at[d, at],
-                    recv_sem=modes_rsem.at[d, at],
-                    device_id={"zbin": lax.rem(z + d, zbins)},
-                    device_id_type=MESH,
-                )
-                copy.start()
-                modes_copies[d, at] = copy
+        for b in range(bins):
+            cols_copies[d, b].wait_recv()
+            for at in range(blocks):
+                second_transform(d, b, at, modes_send if d else modes)
+                if d:
+                    part = pl.ds(0, heights[at])
+                    copy = pltpu.make_async_remote_copy(
+                        src_ref=modes_send.at[d, at, b, :, part, :],
+                        dst_ref=modes.at[d, at, b, :, part, :],
+                        send_sem=modes_ssem.at[d, b * blocks + at],
+                        recv_sem=modes_rsem.at[d, b * blocks + at],
+                        device_id={"zbin": lax.rem(z + d, zbins)},
+                        device_id_type=MESH,
+                    )
+                    copy.start()
+                    modes_copies[d, b, at] = copy
 
     bank_copies = []
     for k in range(1, patches):
@@ -275,13 +290,11 @@
         counts = counts + jnp.sum(outer - inner, axis=0, keepdims=True)
 
     for d in range(1, zbins):
-        new = [(d, b) for b in range(bins)]
-        pairs = [(a, c) for a in done for c in new]
-        pairs += [(new[i], new[j]) for i in range(bins) for j in range(i, bins)]
-        for at in range(blocks):
-            modes_copies[d, at].wait_recv()
-            band_sums(at, pairs)
-        done += new
+        for b in range(bins):
+            done.append((d, b))
+            for at in range(blocks):
+                modes_copies[d, b, at].wait_recv()
+                band_sums(at, [(old, (d, b)) for old in done])
     loads[3].wait()
 
     copies = []
@@ -335,6 +348,7 @@
     pair_share = bins_total * (bins_total + 1) // 2 // zbins
     padded = -(-pair_share // 8) * 8
     group = zbins * freqs - 1
+    slots = margin_src.shape[1] * W
     blocks = half // LANES
 
     profile = taper_profile(length, APOD)
@@ -371,15 +385,18 @@
             pltpu.VMEM((bins, 4, W, columns), bf16),
             pltpu.VMEM((patches,) + coupling_bank.shape, f32),
             pltpu.VMEM((bins, length, columns), bf16),
-            pltpu.VMEM((zbins, bins * 2 * rows, columns), bf16),
-            pltpu.VMEM((zbins, bins * 2 * rows, columns), bf16),
-            pltpu.VMEM((zbins, bins * 2 * rows, columns), bf16),
+            pltpu.VMEM((2, bins, 2 * rows, columns), f32),
+            pltpu.VMEM((length, slots), bf16),
+            pltpu.VMEM((bins, slots, columns), bf16),
+            pltpu.VMEM((zbins, bins, 2 * rows, columns), bf16),
+            pltpu.VMEM((zbins, bins, 2 * rows, columns), bf16),
+            pltpu.VMEM((zbins, bins, 2 * rows, columns), bf16),
             pltpu.VMEM((zbins, blocks, bins, 4, rows, LANES), bf16),
             pltpu.VMEM((zbins, blocks, bins, 4, rows, LANES), bf16),
             pltpu.VMEM((zbins, padded, LANES), f32),
             pltpu.VMEM((group, padded, LANES), f32),
-            dma((4,)), dma((4,)), dma((4,)), dma((patches,)), dma((patches,)), dma((zbins,)), dma((zbins,)),
-            dma((zbins, blocks)), dma((zbins, blocks)), dma((group,)), dma((group,)),
+            dma((4,)), dma((4,)), dma((4,)), dma((patches,)), dma((patches,)), dma((zbins, bins)), dma((zbins, bins)),
+            dma((zbins, bins * blocks)), dma((zbins, bins * blocks)), dma((group,)), dma((group,)),
         ],
         compiler_params=pltpu.CompilerParams(
             collective_id=0, has_side_effects=True, vmem_limit_bytes=56 * 1024 * 1024

time: 44.1 us -> 42.7 us (0.968)
  Pallas kernels: 42.7 us -> 41.2 us
    pallas_call x1, Pallas kernels: 42.7 us -> 41.2 us  [per_device(): pl.pallas_call(lambda *refs: kernel(sizes, *refs), out_shape=jax.ShapeDty...]
where the time goes in v4:
time: 42.7 us; the launch traced here: 42.5 us
  Pallas kernels  41.2 us (96%)
  local copies, waits for them, and re-layouts  1.26 us (3%)
    pallas_call x1, Pallas kernels, per_device(): pl.pallas_call(lambda *refs: kernel(sizes, *refs), out_shape=jax.ShapeDty...  41.2 us
    unnamed x1, local copies, waits for them, and re-layouts  1.26 us

profile of v4, /device:TPU:0, one launch (start us, length us, event | category | flops | bytes accessed | tf_op | source)
XLA Modules:
  0.0 42.5 jit_solution(5824329216115005061)
XLA Ops:
  0.0 41.2 %spectra.1 = f32[5,1,128]{2,1,0:T(1,128)} custom-call(s32[4,4]{1,0:T(4,128)} %refs_0_.1, s32[4,4]{1,0:T(4,128)} %refs_1_.1, s32[4]{0:T(128)} %refs_2_.1, s32[4]{0:T(128)} %refs_3_.1, s32[129]{0:T(256)} %refs_4_.1, f32[128,1]{1,0:T(8,128)} %constant.10.clone.refs_5_, f32[1,1024]{1,0:T(1,128)} %constant.17.refs_6_, bf16[256,128]{1,0:T(8,128)(2,1)} %constant.12.clone.refs_7_, ...), custom_call_target="tpu_custom_call" | custom-call | tf_op jit(solution)/shard_map/spectra/pallas_call | solution.py:376
  41.3 1.3 %copy.14 = f32[1,5,128]{2,0,1:T(1,128)} copy(f32[1,5,128]{2,0,1:T(1,128)} %bitcast.1) | data formatting | bytes 5120

commit v5 on v4

--- a/solution.py
+++ b/solution.py
@@ -66,12 +66,12 @@
     right, left = lax.rem(me + 1, patches), lax.rem(me + patches - 1, patches)
 
     loads = [
-        pltpu.make_async_copy(maps_hbm.at[0], maps, load_sem.at[0]),
-        pltpu.make_async_copy(table_hbm, table, load_sem.at[1]),
-        pltpu.make_async_copy(turn_hbm, turn, load_sem.at[2]),
-        pltpu.make_async_copy(bank_hbm, bank.at[0], load_sem.at[3]),
+        pltpu.make_async_copy(table_hbm, table, load_sem.at[0]),
+        pltpu.make_async_copy(turn_hbm, turn, load_sem.at[1]),
+        pltpu.make_async_copy(bank_hbm, bank.at[0], load_sem.at[2]),
     ]
-    for load in loads:
+    map_loads = [pltpu.make_async_copy(maps_hbm.at[0, b], maps.at[b], load_sem.at[3 + b]) for b in range(bins)]
+    for load in map_loads[:1] + loads[:1] + map_loads[1:] + loads[1:]:
         load.start()
 
     group = [(dz, df) for dz in range(zbins) for df in range(freqs) if (dz, df) != (0, 0)]
@@ -87,20 +87,21 @@
         )
     pl.semaphore_wait(barrier, patches - 1 + len(group))
 
-    strip_copies = []
-    for side, target in ((0, right), (1, left)):
-        for s, at in ((0, 0), (1, length - W)):
-            slot = side * 2 + s
-            copy = pltpu.make_async_remote_copy(
-                src_ref=maps_hbm.at[0, :, pl.ds(at, W), :],
-                dst_ref=strips.at[:, slot],
-                send_sem=strip_send.at[slot],
-                recv_sem=strip_recv.at[slot],
-                device_id={"patch": target},
-                device_id_type=MESH,
-            )
-            copy.start()
-            strip_copies.append(copy)
+    strip_copies = {b: [] for b in range(bins)}
+    for b in range(bins):
+        for side, target in ((0, right), (1, left)):
+            for half_side, at in ((0, 0), (1, length - W)):
+                slot = side * 2 + half_side
+                copy = pltpu.make_async_remote_copy(
+                    src_ref=maps_hbm.at[0, b, pl.ds(at, W), :],
+                    dst_ref=strips[b].at[slot],
+                    send_sem=strip_send.at[b, slot],
+                    recv_sem=strip_recv.at[b, slot],
+                    device_id={"patch": target},
+                    device_id_type=MESH,
+                )
+                copy.start()
+                strip_copies[b].append(copy)
 
     discs[...] = jnp.zeros_like(discs)
     entries = []
@@ -116,11 +117,12 @@
         return rows_at
 
     slots = len(entries) * W
-    loads[0].wait()
     col_taper = col_taper_ref[:, pl.ds(pl.multiple_of(f * columns, columns), columns)]
     bounds = [0, APOD] + list(range(4 * APOD, length - APOD, 4 * APOD)) + [length - APOD, length]
-    for start, stop in zip(bounds[:-1], bounds[1:]):
-        for b in range(bins):
+
+    def taper(b):
+        map_loads[b].wait()
+        for start, stop in zip(bounds[:-1], bounds[1:]):
             image = maps[b, pl.ds(start, stop - start), :].astype(jnp.float32)
             if start == 0:
                 image = image * ramp_ref[pl.ds(0, APOD), :]
@@ -135,8 +137,6 @@
         BLOCK * sum((at * LANES) ** 2 + (t * spread) ** 2 < (half - 1) ** 2 for t in range(rows // BLOCK))
         for at in range(blocks)
     ]
-    loads[1].wait()
-
     def rows_of(ref, half_index, d):
         base = half_index * rows_freq + lax.rem(z + d, zbins) * rows
         return jnp.concatenate(
@@ -153,23 +153,28 @@
     def strip_product(half_index, d, b):
         return jnp.dot(rows_of(strip_table, half_index, d), strip_rows[b], preferred_element_type=jnp.float32)
 
+    def prepare(b):
+        taper(b)
+        if b == 0:
+            loads[0].wait()
+        for part, half_index in enumerate((other, f)):
+            waiting[part, b] = base_product(half_index, early, b)
+
+    def take_strips(b):
+        for copy in strip_copies[b]:
+            copy.wait_recv()
+        for k, (slot, _, _) in enumerate(entries):
+            strip = strips[b][slot].astype(jnp.float32) * strip_taper[k * W : (k + 1) * W]
+            strip_rows[b, pl.ds(k * W, W), :] = (strip * col_taper).astype(jnp.bfloat16)
+
     early = order[0]
-    for part, half_index in enumerate((other, f)):
-        for b in range(bins):
-            waiting[part, b] = base_product(half_index, early, b)
+    across = lax.broadcasted_iota(jnp.int32, (slots, length), 1)
+    found = across == entry_rows((slots, 1), 0)
+    strip_taper = jnp.sum(jnp.where(found, col_taper_ref[...], 0.0), axis=1, keepdims=True)
+    prepare(0)
     pixel = lax.broadcasted_iota(jnp.int32, (length, slots), 0)
     pick = (pixel == entry_rows((1, slots), 1)).astype(jnp.float32).astype(jnp.bfloat16)
     strip_table[...] = jnp.dot(table[...], pick, preferred_element_type=jnp.float32).astype(jnp.bfloat16)
-    across = lax.broadcasted_iota(jnp.int32, (slots, length), 1)
-    found = across == entry_rows((slots, 1), 0)
-    strip_taper = jnp.sum(jnp.where(found, col_taper_ref[...], 0.0), axis=1, keepdims=True)
-
-    for copy in strip_copies:
-        copy.wait_recv()
-    for b in range(bins):
-        for k, (slot, _, _) in enumerate(entries):
-            strip = strips[b, slot].astype(jnp.float32) * strip_taper[k * W : (k + 1) * W]
-            strip_rows[b, pl.ds(k * W, W), :] = (strip * col_taper).astype(jnp.bfloat16)
 
     def second_transform(d, b, at, target):
         own = pl.ds(pl.multiple_of(f * columns, columns), columns)
@@ -198,32 +203,40 @@
         copy.start()
         cols_copies[d, b] = copy
 
+    def exchange_cols(d, b):
+        base = waiting[0, b] if d == early else base_product(other, d, b)
+        cols_send[d, b] = (base + strip_product(other, d, b)).astype(jnp.bfloat16)
+        send_cols(d, b)
+        base = waiting[1, b] if d == early else base_product(f, d, b)
+        cols_own[d, b] = (base + strip_product(f, d, b)).astype(jnp.bfloat16)
+
+    def make_modes(d, b):
+        cols_copies[d, b].wait_recv()
+        for at in range(blocks):
+            second_transform(d, b, at, modes_send if d else modes)
+            if d:
+                part = pl.ds(0, heights[at])
+                copy = pltpu.make_async_remote_copy(
+                    src_ref=modes_send.at[d, at, b, :, part, :],
+                    dst_ref=modes.at[d, at, b, :, part, :],
+                    send_sem=modes_ssem.at[d, b * blocks + at],
+                    recv_sem=modes_rsem.at[d, b * blocks + at],
+                    device_id={"zbin": lax.rem(z + d, zbins)},
+                    device_id_type=MESH,
+                )
+                copy.start()
+                modes_copies[d, b, at] = copy
+
     for d in order:
         for b in range(bins):
-            base = waiting[0, b] if d == early else base_product(other, d, b)
-            cols_send[d, b] = (base + strip_product(other, d, b)).astype(jnp.bfloat16)
-            send_cols(d, b)
-        for b in range(bins):
-            base = waiting[1, b] if d == early else base_product(f, d, b)
-            cols_own[d, b] = (base + strip_product(f, d, b)).astype(jnp.bfloat16)
-        if d == early:
-            loads[2].wait()
-        for b in range(bins):
-            cols_copies[d, b].wait_recv()
-            for at in range(blocks):
-                second_transform(d, b, at, modes_send if d else modes)
-                if d:
-                    part = pl.ds(0, heights[at])
-                    copy = pltpu.make_async_remote_copy(
-                        src_ref=modes_send.at[d, at, b, :, part, :],
-                        dst_ref=modes.at[d, at, b, :, part, :],
-                        send_sem=modes_ssem.at[d, b * blocks + at],
-                        recv_sem=modes_rsem.at[d, b * blocks + at],
-                        device_id={"zbin": lax.rem(z + d, zbins)},
-                        device_id_type=MESH,
-                    )
-                    copy.start()
-                    modes_copies[d, b, at] = copy
+            if d == early:
+                take_strips(b)
+            exchange_cols(d, b)
+            if d == early and b + 1 < bins:
+                prepare(b + 1)
+            if d == early and b == 0:
+                loads[1].wait()
+            make_modes(d, b)
 
     bank_copies = []
     for k in range(1, patches):
@@ -295,7 +308,7 @@
             for at in range(blocks):
                 modes_copies[d, b, at].wait_recv()
                 band_sums(at, [(old, (d, b)) for old in done])
-    loads[3].wait()
+    loads[2].wait()
 
     copies = []
     for n, (dz, df) in enumerate(group):
@@ -333,7 +346,7 @@
     for q in range(pair_share):
         out_ref[q] = result[q : q + 1]
 
-    for copy in strip_copies + bank_copies + list(cols_copies.values()) + list(modes_copies.values()) + copies:
+    for copy in sum(strip_copies.values(), []) + bank_copies + list(cols_copies.values()) + list(modes_copies.values()) + copies:
         copy.wait_send()
 
 
@@ -382,7 +395,7 @@
             pltpu.VMEM((bins, length, columns), bf16),
             pltpu.VMEM((length, length), bf16),
             pltpu.VMEM((blocks, length, 2 * LANES), bf16),
-            pltpu.VMEM((bins, 4, W, columns), bf16),
+            [pltpu.VMEM((4, W, columns), bf16)] * bins,
             pltpu.VMEM((patches,) + coupling_bank.shape, f32),
             pltpu.VMEM((bins, length, columns), bf16),
             pltpu.VMEM((2, bins, 2 * rows, columns), f32),
@@ -395,7 +408,7 @@
             pltpu.VMEM((zbins, blocks, bins, 4, rows, LANES), bf16),
             pltpu.VMEM((zbins, padded, LANES), f32),
             pltpu.VMEM((group, padded, LANES), f32),
-            dma((4,)), dma((4,)), dma((4,)), dma((patches,)), dma((patches,)), dma((zbins, bins)), dma((zbins, bins)),
+            dma((3 + bins,)), dma((bins, 4)), dma((bins, 4)), dma((patches,)), dma((patches,)), dma((zbins, bins)), dma((zbins, bins)),
             dma((zbins, bins * blocks)), dma((zbins, bins * blocks)), dma((group,)), dma((group,)),
         ],
         compiler_params=pltpu.CompilerParams(

time: 42.7 us -> 41.3 us (0.967)
  Pallas kernels: 41.2 us -> 39.9 us
    pallas_call x1, Pallas kernels: 41.2 us -> 39.9 us  [per_device(): pl.pallas_call(lambda *refs: kernel(sizes, *refs), out_shape=jax.ShapeDty...]
where the time goes in v5:
time: 41.3 us; the launch traced here: 41.2 us
  Pallas kernels  39.9 us (97%)
  local copies, waits for them, and re-layouts  1.26 us (3%)
    pallas_call x1, Pallas kernels, per_device(): pl.pallas_call(lambda *refs: kernel(sizes, *refs), out_shape=jax.ShapeDty...  39.9 us
    unnamed x1, local copies, waits for them, and re-layouts  1.26 us

profile of v5, /device:TPU:0, one launch (start us, length us, event | category | flops | bytes accessed | tf_op | source)
XLA Modules:
  0.0 41.2 jit_solution(11213366950476198333)
XLA Ops:
  0.0 39.9 %spectra.1 = f32[5,1,128]{2,1,0:T(1,128)} custom-call(s32[4,4]{1,0:T(4,128)} %refs_0_.1, s32[4,4]{1,0:T(4,128)} %refs_1_.1, s32[4]{0:T(128)} %refs_2_.1, s32[4]{0:T(128)} %refs_3_.1, s32[129]{0:T(256)} %refs_4_.1, f32[128,1]{1,0:T(8,128)} %constant.10.clone.refs_5_, f32[1,1024]{1,0:T(1,128)} %constant.17.refs_6_, bf16[256,128]{1,0:T(8,128)(2,1)} %constant.12.clone.refs_7_, ...), custom_call_target="tpu_custom_call" | custom-call | tf_op jit(solution)/shard_map/spectra/pallas_call | solution.py:389
  39.9 1.3 %copy.14 = f32[1,5,128]{2,0,1:T(1,128)} copy(f32[1,5,128]{2,0,1:T(1,128)} %bitcast.1) | data formatting | bytes 5120

commit v6 on v5

--- a/solution.py
+++ b/solution.py
@@ -232,11 +232,11 @@
             if d == early:
                 take_strips(b)
             exchange_cols(d, b)
-            if d == early and b + 1 < bins:
-                prepare(b + 1)
             if d == early and b == 0:
                 loads[1].wait()
             make_modes(d, b)
+            if d == early and b + 1 < bins:
+                prepare(b + 1)
 
     bank_copies = []
     for k in range(1, patches):

time: 41.3 us -> 40.1 us (0.971)
  Pallas kernels: 39.9 us -> 38.6 us
    pallas_call x1, Pallas kernels: 39.9 us -> 38.6 us  [per_device(): pl.pallas_call(lambda *refs: kernel(sizes, *refs), out_shape=jax.ShapeDty...]
where the time goes in v6:
time: 40.1 us; the launch traced here: 39.9 us
  Pallas kernels  38.6 us (96%)
  local copies, waits for them, and re-layouts  1.26 us (3%)
    pallas_call x1, Pallas kernels, per_device(): pl.pallas_call(lambda *refs: kernel(sizes, *refs), out_shape=jax.ShapeDty...  38.6 us
    unnamed x1, local copies, waits for them, and re-layouts  1.26 us

profile of v6, /device:TPU:0, one launch (start us, length us, event | category | flops | bytes accessed | tf_op | source)
XLA Modules:
  0.0 39.9 jit_solution(6816415014881558305)
XLA Ops:
  0.0 38.6 %spectra.1 = f32[5,1,128]{2,1,0:T(1,128)} custom-call(s32[4,4]{1,0:T(4,128)} %refs_0_.1, s32[4,4]{1,0:T(4,128)} %refs_1_.1, s32[4]{0:T(128)} %refs_2_.1, s32[4]{0:T(128)} %refs_3_.1, s32[129]{0:T(256)} %refs_4_.1, f32[128,1]{1,0:T(8,128)} %constant.10.clone.refs_5_, f32[1,1024]{1,0:T(1,128)} %constant.17.refs_6_, bf16[256,128]{1,0:T(8,128)(2,1)} %constant.12.clone.refs_7_, ...), custom_call_target="tpu_custom_call" | custom-call | tf_op jit(solution)/shard_map/spectra/pallas_call | solution.py:389
  38.6 1.3 %copy.14 = f32[1,5,128]{2,0,1:T(1,128)} copy(f32[1,5,128]{2,0,1:T(1,128)} %bitcast.1) | data formatting | bytes 5120

commit v7 on v6

--- a/solution.py
+++ b/solution.py
@@ -176,10 +176,13 @@
     pick = (pixel == entry_rows((1, slots), 1)).astype(jnp.float32).astype(jnp.bfloat16)
     strip_table[...] = jnp.dot(table[...], pick, preferred_element_type=jnp.float32).astype(jnp.bfloat16)
 
-    def second_transform(d, b, at, target):
+    def near_product(d, b, at):
         own = pl.ds(pl.multiple_of(f * columns, columns), columns)
+        return jnp.dot(cols_own[d, b], turn[at, own, :], preferred_element_type=jnp.float32)
+
+    def second_transform(d, b, at, target, near):
         far = pl.ds(pl.multiple_of(other * columns, columns), columns)
-        both = jnp.dot(cols_own[d, b], turn[at, own, :], preferred_element_type=jnp.float32) + jnp.dot(
+        both = near + jnp.dot(
             cols_recv[d, b], turn[at, far, :], preferred_element_type=jnp.float32
         )
         real_cos, real_sin = both[:rows, :LANES], both[:rows, LANES:]
@@ -211,9 +214,12 @@
         cols_own[d, b] = (base + strip_product(f, d, b)).astype(jnp.bfloat16)
 
     def make_modes(d, b):
+        near = near_product(d, b, 0)
         cols_copies[d, b].wait_recv()
         for at in range(blocks):
-            second_transform(d, b, at, modes_send if d else modes)
+            if at:
+                near = near_product(d, b, at)
+            second_transform(d, b, at, modes_send if d else modes, near)
             if d:
                 part = pl.ds(0, heights[at])
                 copy = pltpu.make_async_remote_copy(

time: 40.1 us -> 40.1 us (level)
  no operation moved by 1% of the time
where the time goes in v7:
time: 40.1 us; the launch traced here: 39.9 us
  Pallas kernels  38.7 us (97%)
  local copies, waits for them, and re-layouts  1.26 us (3%)
    pallas_call x1, Pallas kernels, per_device(): pl.pallas_call(lambda *refs: kernel(sizes, *refs), out_shape=jax.ShapeDty...  38.7 us
    unnamed x1, local copies, waits for them, and re-layouts  1.26 us

profile of v7, /device:TPU:0, one launch (start us, length us, event | category | flops | bytes accessed | tf_op | source)
XLA Modules:
  0.0 39.9 jit_solution(17385737151464204820)
XLA Ops:
  0.0 38.7 %spectra.1 = f32[5,1,128]{2,1,0:T(1,128)} custom-call(s32[4,4]{1,0:T(4,128)} %refs_0_.1, s32[4,4]{1,0:T(4,128)} %refs_1_.1, s32[4]{0:T(128)} %refs_2_.1, s32[4]{0:T(128)} %refs_3_.1, s32[129]{0:T(256)} %refs_4_.1, f32[128,1]{1,0:T(8,128)} %constant.10.clone.refs_5_, f32[1,1024]{1,0:T(1,128)} %constant.17.refs_6_, bf16[256,128]{1,0:T(8,128)(2,1)} %constant.12.clone.refs_7_, ...), custom_call_target="tpu_custom_call" | custom-call | tf_op jit(solution)/shard_map/spectra/pallas_call | solution.py:395
  38.7 1.3 %copy.14 = f32[1,5,128]{2,0,1:T(1,128)} copy(f32[1,5,128]{2,0,1:T(1,128)} %bitcast.1) | data formatting | bytes 5120
